TPU v7x, 256 devices: a whole 4x4x8 slice. The times are simulated.
256 devices in a mesh: ctx: 64 (over z_lo, x, y), tp: 4 (over z_hi, core).
Axes of the slice: x: 4, y: 4, z: 8 (z_hi: 2, z_lo: 4; z = z_hi * 4 + z_lo), core: 2. Of those that a mesh axis runs over, the one named last changes fastest.
Arguments:
- step_inputs: bfloat16 [8192, 8192], P('ctx', 'tp'), may hold values from -6 to 6
- log_decay: float32 [8192, 128], P('ctx', 'tp'), may hold values from -0.7 to 0
- write_vecs: bfloat16 [8192, 2048], P('ctx', 'tp'), may hold values from -6 to 6
- read_vecs: bfloat16 [8192, 2048], P('ctx', 'tp'), may hold values from -0.375 to 0.375
- gate_vals: bfloat16 [8192, 8192], P('ctx', 'tp'), may hold values from -6 to 6
- skip_gain: float32 [128], P('tp'), may hold values from 0.5 to 2
- norm_gain: float32 [8192], P('tp'), may hold values from 0.5 to 1.5
- query_rows: bfloat16 [8192, 4096], P('ctx', 'tp'), may hold values from -160 to 160
- key_rows: bfloat16 [8192, 1024], P('ctx', 'tp'), may hold values from -6 to 6
- value_rows: bfloat16 [8192, 1024], P('ctx', 'tp'), may hold values from -6 to 6
Outputs:
- mamba_out: bfloat16 [8192, 8192], P('ctx', 'tp')
- attn_out: bfloat16 [8192, 4096], P('ctx', 'tp')
All inputs are finite; a program needn't handle non-finite values.
Results may differ from a plain program's by a relative error of at most 0.0049.
Values may be sent and summed in bfloat16 or wider, within the bound.
No kernel may reach another device: no remote copies, remote signals or barrier semaphores. Data moves between devices by JAX's collectives and lax.ppermute only.
A program may use at most 320 MiB of HBM per device.

v0:
```python
import functools

import jax
import jax.numpy as jnp
from jax import lax
from jax.experimental import pallas as pl
from jax.experimental.pallas import tpu as pltpu
from jax.sharding import PartitionSpec as P

MHDIM = 64
NSTATE = 256
HDIM = 128
LBLK = 128
SLICE = 512
KVW = 2 * HDIM
AT_B = SLICE
AT_C = AT_B + NSTATE
AT_DECAY = AT_C + NSTATE
WIDTH = AT_DECAY + 128

eps_norm = 1e-05
neg_large = -1e30
no_top = -1e29
score_scale = HDIM ** (-0.5) * 1.4426950408889634

bf16 = jnp.bfloat16
f32 = jnp.float32


def shape(dims, dtype):
    return jax.ShapeDtypeStruct(dims, dtype)


def run(kernel, outs, args, scratch=(), flops=1000000, moved=1000000, aliases=None, after=()):
    vmem = pl.BlockSpec(memory_space=pltpu.VMEM)
    smem = pl.BlockSpec(memory_space=pltpu.SMEM)
    held = len(args)

    def body(*refs):
        kernel(*refs[:held], *refs[held + len(after) :])

    return pl.pallas_call(
        body if after else kernel,
        out_shape=outs,
        in_specs=[smem] + [vmem] * (held - 1) + [pl.BlockSpec(memory_space=pl.ANY)] * len(after),
        out_specs=[vmem] * len(outs),
        scratch_shapes=list(scratch),
        input_output_aliases=aliases or {},
        compiler_params=pltpu.CompilerParams(vmem_limit_bytes=24 * 1024 * 1024),
        cost_estimate=pl.CostEstimate(flops=flops, bytes_accessed=moved, transcendentals=0),
    )(*args, *after)


def ring4(place, shift):
    return lax.bitwise_and(place + shift, 3)


def lanes(start, size):
    return pl.ds(pl.multiple_of(start * size, size), size)


def split3(vals):
    high = vals.astype(bf16)
    rest = vals - high.astype(f32)
    mid = rest.astype(bf16)
    low = (rest - mid.astype(f32)).astype(bf16)
    return high, mid, low


def iota(dims, dim):
    return lax.broadcasted_iota(jnp.int32, dims, dim)


def pack_kernel(decay, x, b, c, *outs):
    y = lax.bitwise_and(lax.axis_index("ctx").astype(jnp.int32), 3)
    lane = iota((LBLK, 128), 1)
    for s, out in enumerate(outs):
        j = ring4(y, s)
        group = lax.shift_right_logical(j, 1)
        out[:, 0:SLICE] = x[:, lanes(j, SLICE)]
        out[:, AT_B:AT_C] = b[:, lanes(group, NSTATE)]
        out[:, AT_C:AT_DECAY] = c[:, lanes(group, NSTATE)]
        high, mid, low = (part.astype(f32) for part in split3(decay[:, lanes(j, 128)]))
        out[:, AT_DECAY:] = jnp.where(lane < 8, high, jnp.where(lane < 16, mid, low)).astype(bf16)


def pair_kernel(place, own, swapped, out):
    out[0:LBLK, :] = own[...]
    out[LBLK:, :] = swapped[:, :KVW]


def write_total(out, state, log_total):
    out[0:NSTATE, :] = state.astype(bf16)
    high, mid, low = split3(log_total)
    row = iota((16, log_total.shape[1]), 0)
    out[NSTATE:, :] = jnp.where(
        row == 0,
        high.astype(f32),
        jnp.where(row == 1, mid.astype(f32), jnp.where(row == 2, low.astype(f32), 0.0)),
    ).astype(bf16)


def read_total(vals):
    tail = vals[NSTATE:, :].astype(f32)
    return vals[0:NSTATE, :].astype(f32), tail[0:1] + tail[1:2] + tail[2:3]


def total_kernel(place, r0, r1, r2, r3, t0, t1, t2, t3, ordered, cums, states, total):
    x, y = place[1], place[2]
    for s, r in enumerate((r0, r1, r2, r3)):
        ordered[ring4(y, -s)] = r[...]
    tri = (iota((LBLK, LBLK), 0) >= iota((LBLK, LBLK), 1)).astype(f32).astype(bf16)
    cum_parts = jnp.concatenate(
        [jnp.dot(tri, ordered[block, :, AT_DECAY:], preferred_element_type=f32) for block in range(4)], axis=0
    )
    row = iota((128, SLICE), 0)
    head = lax.shift_right_logical(iota((128, SLICE), 1), 6)
    spread = jnp.where((lax.bitwise_and(row, 7) == head) & (row < 24), 1.0, 0.0).astype(bf16)
    cum_all = functools.reduce(
        jnp.add, [jnp.dot(part, spread, preferred_element_type=f32) for part in split3(cum_parts)]
    )
    log_total = jnp.zeros((1, SLICE), f32)
    for block in range(4):
        cum = cum_all[block * LBLK : (block + 1) * LBLK]
        last = cum[LBLK - 1 : LBLK, :]
        cums[block] = cum
        decayed = (ordered[block, :, 0:SLICE].astype(f32) * jnp.exp(last - cum)).astype(bf16)
        state = lax.dot_general(
            ordered[block, :, AT_B:AT_C], decayed, (((0,), (0,)), ((), ())), preferred_element_type=f32
        )
        states[block] = state
        log_total = log_total + last
        total[...] = state if block == 0 else jnp.exp(last) * total[...] + state
    for s, t in enumerate((t0, t1, t2, t3)):
        j = ring4(x, s)
        log_part = jnp.where(
            j == 0,
            log_total[:, 0:128],
            jnp.where(j == 1, log_total[:, 128:256], jnp.where(j == 2, log_total[:, 256:384], log_total[:, 384:512])),
        )
        write_total(t, total[:, lanes(j, 128)], log_part)


def local_kernel(place, ordered, cums, states, skip, local, decay, held):
    gain = skip[:, lanes(place[2], SLICE)]
    causal = iota((LBLK, LBLK), 0) >= iota((LBLK, LBLK), 1)
    tri = causal.astype(f32).astype(bf16)
    low_half = iota((LBLK, 128), 1) < MHDIM
    before = jnp.zeros((1, SLICE), f32)
    for block in range(4):
        cum = cums[block]
        last = cum[LBLK - 1 : LBLK, :]
        decay[block] = jnp.exp(cum + before)
        before = before + last
        parts = ordered[block, :, AT_DECAY:]
        row_parts = lax.dot_general(parts, tri, (((0,), (1,)), ((), ())), preferred_element_type=f32)
        cum_rows = row_parts[0:8] + row_parts[8:16] + row_parts[16:24]
        read = ordered[block, :, AT_C:AT_DECAY]
        pair_dots = lax.dot_general(
            read, ordered[block, :, AT_B:AT_C], (((1,), (1,)), ((), ())), preferred_element_type=f32
        )
        if block == 0:
            held[...] = states[0]
        else:
            state = held[...]
            high = state.astype(bf16)
            low = (state - high.astype(f32)).astype(bf16)
            inflow = jnp.dot(read, high, preferred_element_type=f32) + jnp.dot(read, low, preferred_element_type=f32)
            if block < 3:
                held[...] = jnp.exp(last) * state + states[block]
        for pair in range(4):
            part = slice(pair * 128, pair * 128 + 128)
            xs = ordered[block, :, part]
            sums = []
            for head in (2 * pair, 2 * pair + 1):
                gap = cum[:, head * MHDIM : head * MHDIM + 1] - cum_rows[head : head + 1, :]
                weight = (jnp.exp(jnp.where(causal, gap, neg_large)) * pair_dots).astype(bf16)
                sums.append(jnp.dot(weight, xs, preferred_element_type=f32))
            vals = jnp.where(low_half, sums[0], sums[1]) + gain[:, part] * xs.astype(f32)
            if block > 0:
                vals = vals + jnp.exp(cum[:, part]) * inflow[:, part]
            local[block, :, part] = vals


def plane_kernel(place, r0, r1, r2, r3, column, out, later_column, ordered):
    x = place[1]
    later_column[...] = column[...]
    for s, r in enumerate((r0, r1, r2, r3)):
        ordered[ring4(x, -s)] = r[...]
    total, log_total = read_total(ordered[0])
    for block in range(1, 4):
        state, last = read_total(ordered[block])
        total = jnp.exp(last) * total + state
        log_total = log_total + last
    write_total(out, total, log_total)


def entering_kernel(place, r0, r1, r2, r3, up1, up2, up3, g0, g1, g2, g3, ordered, entering):
    x = place[1]
    for s, r in enumerate((r0, r1, r2, r3)):
        ordered[ring4(x, -s)] = r[...]
    current = jnp.zeros((NSTATE, 128), f32)
    for distance, up in ((3, up3), (2, up2), (1, up1)):
        state, last = read_total(up[...])
        current = jnp.where(place[0] >= distance, jnp.exp(last) * current + state, 0.0)
    for block in range(4):
        entering[block] = current.astype(bf16)
        if block < 3:
            state, last = read_total(ordered[block])
            current = jnp.exp(last) * current + state
    for s, g in enumerate((g0, g1, g2, g3)):
        g[...] = entering[ring4(x, s)]


def mixed_kernel(place, ordered, local, decay, g0, g1, g2, g3, m0, m1, m2, m3, carried, results):
    x, y = place[1], place[2]
    for s, g in enumerate((g0, g1, g2, g3)):
        carried[:, lanes(ring4(x, -s), 128)] = g[...]
    for block in range(4):
        inflow = jnp.dot(ordered[block, :, AT_C:AT_DECAY], carried[...], preferred_element_type=f32)
        results[block] = (local[block] + decay[block] * inflow).astype(bf16)
    for s, m in enumerate((m0, m1, m2, m3)):
        m[...] = results[ring4(y, s)]


def silu_kernel(place, gate, out):
    gates = gate[...].astype(f32)
    out[...] = gates / (1.0 + jnp.exp(-gates))


def norm_kernel(place, m0, m1, m2, m3, gates, gain, out):
    y = place[2]
    gated, squares, groups, slots = [], [], [], []
    for s, m in enumerate((m0, m1, m2, m3)):
        j = ring4(y, -s)
        vals = m[...].astype(f32) * gates[:, lanes(j, SLICE)]
        gated.append(vals)
        squares.append(jnp.sum(vals * vals, axis=1, keepdims=True))
        groups.append(lax.shift_right_logical(j, 1))
        slots.append(j)
    for s in range(4):
        total = jnp.zeros((LBLK, 1), f32)
        for other in range(4):
            total = total + jnp.where(groups[other] == groups[s], squares[other], 0.0)
        factor = lax.rsqrt(total * (1.0 / 1024.0) + eps_norm)
        out[:, lanes(slots[s], SLICE)] = (gated[s] * factor * gain[:, lanes(slots[s], SLICE)]).astype(bf16)


def query_tile(queries, tile):
    one, head = queries[tile // 4], tile % 4
    start = one.shape[1] - (4 - head) * HDIM
    return one[:, start : start + HDIM]


def with_ones(value):
    return jnp.concatenate([value, jnp.ones_like(value)], axis=1)


def attend(tile, queries, keys, values, state, limit=None):
    tops, sums, acc = state
    rows = slice(tile * LBLK, (tile + 1) * LBLK)
    scores = [
        lax.dot_general(queries, key, (((1,), (1,)), ((), ())), preferred_element_type=f32) for key in keys
    ]
    if limit is not None:
        scores = limit(scores)
    top = functools.reduce(jnp.maximum, scores)
    held_top = tops[rows, 0:1]
    new_top = jnp.maximum(held_top, jnp.max(top, axis=1, keepdims=True))
    expos = [jnp.exp2((score - new_top) * score_scale).astype(bf16) for score in scores]
    factor = jnp.exp2((held_top - new_top) * score_scale)
    summed = functools.reduce(
        jnp.add, [jnp.dot(expo, value, preferred_element_type=f32) for expo, value in zip(expos, values)]
    )
    tops[rows, :] = jnp.broadcast_to(new_top, (LBLK, 128))
    sums[rows, :] = sums[rows, :] * factor + summed[:, HDIM:]
    acc[rows, :] = acc[rows, :] * factor + summed[:, :HDIM]


def offset(visible):
    return jnp.where(visible, 0.0, neg_large).astype(f32)


def add_offsets(scores, offsets):
    return [score + one for score, one in zip(scores, offsets)]


def every_tile(place, queries, keys, values, state, own_plane):
    offsets = [offset(place[0] >= distance) for distance in (1, 2, 3)]
    for tile in range(16):

        def limit(scores, slot=tile // 4):
            return [own_plane(scores[0], slot)] + add_offsets(scores[1:], offsets)

        attend(tile, query_tile(queries, tile), keys, values, state, limit)


def own_kernel(place, q0, q1, q2, q3, kv0, kv1, kv2, kv3, tops, sums, acc):
    x = place[1]
    tops[...] = jnp.full(tops.shape, no_top, f32)
    sums[...] = jnp.zeros(sums.shape, f32)
    acc[...] = jnp.zeros(acc.shape, f32)
    blocks = (kv0, kv1, kv2, kv3)
    keys = [kv[:, :HDIM] for kv in blocks]
    values = [with_ones(kv[:, HDIM:]) for kv in blocks]
    lane = iota((LBLK, KVW), 1)
    key_pos = jnp.where(lane < LBLK, x, lax.bitwise_xor(x, 1)) * LBLK + lax.bitwise_and(lane, LBLK - 1)
    ahead = key_pos - iota((LBLK, KVW), 0)

    def own_plane(score, slot):
        return jnp.where(ahead <= lax.bitwise_xor(x, slot) * LBLK, score, neg_large)

    every_tile(place, (q0, q1, q2, q3), keys, values, (tops, sums, acc), own_plane)


def column_attend(step, place, q0, q1, q2, q3, old_tops, old_sums, old_acc, *refs):
    column, outs = refs[0], refs[1:]
    state = outs[:3]
    x, y = place[1], place[2]
    other = ring4(y, step)
    blocks = [column[plane * KVW : (plane + 1) * KVW, :] for plane in range(4)]
    keys = [kv[:, :HDIM] for kv in blocks]
    values = [with_ones(kv[:, HDIM:]) for kv in blocks]
    lane = iota((1, KVW), 1)

    def own_plane(score, slot):
        query_block = lax.bitwise_xor(x, slot) * 4 + y
        near, far = (offset(one * 4 + other < query_block) for one in (x, lax.bitwise_xor(x, 1)))
        return score + jnp.where(lane < LBLK, near, far)

    every_tile(place, (q0, q1, q2, q3), keys, values, state, own_plane)
    if step == 2:
        tops, sums, acc = state
        lane = iota((LBLK, 128), 1)
        for s, o in enumerate(outs[3:]):
            stats = jnp.zeros((LBLK, 128), f32)
            for head in range(4):
                start = (s * 4 + head) * LBLK
                rows = slice(start, start + LBLK)
                total = sums[rows, :]
                o[:, head * HDIM : (head + 1) * HDIM] = (acc[rows, :] / jnp.where(total > 0, total, 1.0)).astype(bf16)
                stats = jnp.where(lane == head * 6, tops[rows, :], jnp.where(lane == head * 6 + 3, total, stats))
            high, mid, low = (part.astype(f32) for part in split3(stats))
            o[:, 4 * HDIM :] = (high + pltpu.roll(mid, 1, 1) + pltpu.roll(low, 2, 1)).astype(bf16)


def merge_kernel(place, o0, o1, o2, o3, out):
    head_group = lax.bitwise_and(place[1], 1)
    for pair, group in (((o0, o2), head_group), ((o1, o3), 1 - head_group)):
        tops, sums = [], []
        for part in pair:
            stats = part[:, 4 * HDIM :].astype(f32)
            stats = stats + pltpu.roll(stats, 127, 1) + pltpu.roll(stats, 126, 1)
            tops.append(stats)
            sums.append(pltpu.roll(stats, 125, 1))
        top = jnp.maximum(tops[0], tops[1])
        weights = [total * jnp.exp2(jnp.minimum((one - top) * score_scale, 0.0)) for one, total in zip(tops, sums)]
        whole = weights[0] + weights[1]
        shares = [weight / jnp.where(whole > 0, whole, 1.0) for weight in weights]
        for head in range(4):
            cols = slice(head * HDIM, (head + 1) * HDIM)
            vals = [
                part[:, cols].astype(f32) * share[:, head * 6 : head * 6 + 1] for part, share in zip(pair, shares)
            ]
            start = pl.multiple_of(group * (4 * HDIM) + head * HDIM, HDIM)
            out[:, pl.ds(start, HDIM)] = (vals[0] + vals[1]).astype(bf16)


def shift_y(vals, shift):
    return lax.ppermute(vals, "ctx", [(i, (i & ~3) | ((i + shift) & 3)) for i in range(64)])


def shift_x(vals, shift):
    return lax.ppermute(vals, "ctx", [(i, (i & ~12) | ((i + 4 * shift) & 12)) for i in range(64)])


def swap_x(vals, step):
    return lax.ppermute(vals, "ctx", [(i, i ^ (4 * step)) for i in range(64)])


def up_z(vals, shift):
    return lax.ppermute(vals, "ctx", [(i, (i + 16 * shift) & 63) for i in range(64)])


def on_device(
    step_inputs, log_decay, write_vecs, read_vecs, gate_vals, skip_gain, norm_gain, query_rows, key_rows, value_rows
):
    index = lax.axis_index("ctx").astype(jnp.int32)
    place = jnp.stack([index // 16, (index // 4) % 4, index % 4, index])
    decay_copies = jnp.tile(log_decay.reshape(LBLK, 4, 1, 8), (1, 1, 3, 1)).reshape(LBLK, 4, 24)
    decay_grid = jnp.pad(decay_copies, ((0, 0), (0, 0), (0, 104))).reshape(LBLK, 512)
    skip = jnp.repeat(skip_gain, MHDIM).reshape(1, 4 * SLICE)
    gain = norm_gain.reshape(1, 4 * SLICE)

    head = (index // 4) % 2

    def one_head(group):
        parts = [lax.dynamic_slice_in_dim(rows, group * HDIM, HDIM, 1) for rows in (key_rows, value_rows)]
        return jnp.concatenate(parts, axis=1)

    def its_queries(group):
        return lax.dynamic_slice_in_dim(query_rows, group * (4 * HDIM), 4 * HDIM, 1)

    kv_own, q_same, q_other = one_head(head), its_queries(head), its_queries(1 - head)
    swapped = swap_x(jnp.concatenate([one_head(1 - head), q_other], axis=1), 1)
    vmem = pl.BlockSpec(memory_space=pltpu.VMEM)
    rings = pl.pallas_call(
        pack_kernel,
        out_shape=[shape((LBLK, WIDTH), bf16)] * 4,
        in_specs=[vmem] * 4,
        out_specs=[vmem] * 4,
        compiler_params=pltpu.CompilerParams(vmem_limit_bytes=60 * 1024 * 1024),
    )(decay_grid, step_inputs, write_vecs, read_vecs)
    rings = [rings[0]] + [shift_y(rings[s], s) for s in (1, 2, 3)]

    queries = [q_same, swapped, swap_x(q_same, 2), swap_x(q_other, 3)]

    (kv,) = run(pair_kernel, [shape((2 * LBLK, KVW), bf16)], (place, kv_own, swapped), after=[rings[0]])
    up1, up2 = up_z(kv, 1), up_z(kv, 2)
    ups = [up1, up2, up_z(up2, 1)]
    column = jnp.concatenate([kv] + ups, axis=0)
    left, right = shift_y(column, 1), shift_y(column, -1)

    gates = run(silu_kernel, [shape((LBLK, 4 * SLICE), f32)], (place, gate_vals), moved=2 << 20)[0]
    ring_grid = [shape((4, LBLK, SLICE), f32)] * 2
    *totals, ordered, cums, states = run(
        total_kernel,
        [shape((NSTATE + 16, 128), bf16)] * 4
        + [shape((4, LBLK, WIDTH), bf16), ring_grid[0], shape((4, NSTATE, SLICE), f32)],
        (place, *rings),
        [pltpu.VMEM((NSTATE, SLICE), f32)],
        flops=600 << 20,
        moved=2 << 20,
        after=[ups[2], gates],
    )
    totals = [totals[0]] + [shift_x(totals[s], s) for s in (1, 2, 3)]

    rows = 16 * LBLK
    state_shapes = [shape((rows, 128), f32)] * 3
    out_shapes = [shape((LBLK, 4 * HDIM + 128), bf16)] * 4

    def attend_column(state, step, keys, after=()):
        return run(
            functools.partial(column_attend, step),
            state_shapes + (out_shapes if step == 2 else []),
            (place, *queries, *state, *keys),
            flops=4 << 30,
            moved=8 << 20,
            aliases={5: 0, 6: 1, 7: 2},
            after=after,
        )

    state = run(own_kernel, state_shapes, (place, *queries, kv, *ups), flops=4 << 30, moved=8 << 20, after=[totals[0]])
    plane_total, later_column = run(
        plane_kernel,
        [shape((NSTATE + 16, 128), bf16), shape(column.shape, bf16)],
        (place, *totals, column),
        [pltpu.VMEM((4, NSTATE + 16, 128), bf16)],
        after=[state[1]],
    )
    total_ups = [up_z(plane_total, s) for s in (1, 2, 3)]
    local, decay = run(
        local_kernel,
        ring_grid,
        (place, ordered, cums, states, skip),
        [pltpu.VMEM((NSTATE, SLICE), f32)],
        flops=2 << 30,
        moved=4 << 20,
        after=[plane_total],
    )
    entering = run(
        entering_kernel,
        [shape((NSTATE, 128), bf16)] * 4,
        (place, *totals, *total_ups),
        [pltpu.VMEM((4, NSTATE + 16, 128), bf16), pltpu.VMEM((4, NSTATE, 128), bf16)],
        after=[local],
    )
    state = attend_column(state, -1, [left], [entering[0]])
    entering = [entering[0]] + [shift_x(entering[s], s) for s in (1, 2, 3)]
    mixed = run(
        mixed_kernel,
        [shape((LBLK, SLICE), bf16)] * 4,
        (place, ordered, local, decay, *entering),
        [pltpu.VMEM((NSTATE, SLICE), bf16), pltpu.VMEM((4, LBLK, SLICE), bf16)],
        after=[state[1]],
    )
    state = attend_column(state, 1, [right], [mixed[0]])
    mixed = [mixed[0]] + [shift_y(mixed[s], s) for s in (1, 2, 3)]
    *_, o0, o1, o2, o3 = attend_column(state, 2, [shift_y(later_column, 2)], mixed[1:])
    outs = [o0] + [swap_x(one, s) for s, one in ((1, o1), (2, o2), (3, o3))]
    (mamba_out,) = run(norm_kernel, [shape((LBLK, 4 * SLICE), bf16)], (place, *mixed, gates, gain), after=[o0])
    (attn_out,) = run(merge_kernel, [shape((LBLK, 8 * HDIM), bf16)], (place, *outs))
    return (mamba_out, attn_out)


def solution(mesh):
    in_specs = (
        P("ctx", "tp"),
        P("ctx", "tp"),
        P("ctx", "tp"),
        P("ctx", "tp"),
        P("ctx", "tp"),
        P("tp"),
        P("tp"),
        P("ctx", "tp"),
        P("ctx", "tp"),
        P("ctx", "tp"),
    )
    out_specs = (P("ctx", "tp"), P("ctx", "tp"))
    return jax.shard_map(on_device, mesh=mesh, in_specs=in_specs, out_specs=out_specs, check_vma=False)
```

profile of v0, /device:TPU:8, one launch (start us, length us, event | category | flops | bytes accessed | tf_op | source)
XLA Modules:
  0.0 88.1 jit_solution(12964664566261398278)
XLA Ops:
  0.7 1.0 %constant_dynamic-slice_fusion = (bf16[128,512]{1,0:T(8,128)(2,1)S(1)}, bf16[128,512]{1,0:T(8,128)(2,1)S(1)}) fusion(bf16[128,1024]{1,0:T(8,128)(2,1)} %param.17, s32[]{:T(128)S(6)} %select_n.45, s32[]{:T(128)S(6)} %select_n.44), kind=kLoop, calls=%fused_computation.4 | loop fusion | bytes 524296 | tf_op jit(solution)/shard_map/dynamic_slice | solution.py:402
  1.8 0.8 constant_dynamic-slice_fusion.2
  2.6 1.6 %collective-permute-start.3 = (bf16[128,768]{1,0:T(8,128)(2,1)S(1)}, bf16[128,768]{1,0:T(8,128)(2,1)S(1)}, u32[]{:S(2)}, u32[]{:S(2)}) collective-permute-start(bf16[128,768]{1,0:T(8,128)(2,1)S(1)} %pad_maximum_fusion.1), channel_id=1, source_target_pairs={{0,16},{4,20},{8,24},{12,28},{16,0},{20,4},{24,8},{28,12},{32,48},... | collective-permute-start | bytes 589832 | tf_op jit(solution)/shard_map/ppermute | solution.py:378
  4.2 0.8 copy.23.decay
  5.1 2.3 %shard_map.113 = (bf16[128,1152]{1,0:T(8,128)(2,1)}, bf16[128,1152]{1,0:T(8,128)(2,1)}, bf16[128,1152]{1,0:T(8,128)(2,1)}, bf16[128,1152]{1,0:T(8,128)(2,1)}) custom-call(f32[128,512]{1,0:T(8,128)} %copy.23.decay, bf16[128,2048]{1,0:T(8,128)(2,1)} %x.3, bf16[128,512]{1,0:T(8,128)(2,1)} %b.1, bf16[128,512]{1,0:T(8,128)(2,1)} %c.1), custom_call_target="tpu_custom_call" | custom-call | tf_op jit(solution)/shard_map/pallas_call | solution.py:407
  7.5 1.9 %collective-permute-done.3.refs_2_ = bf16[128,768]{1,0:T(8,128)(2,1)S(1)} collective-permute-done((bf16[128,768]{1,0:T(8,128)(2,1)S(1)}, bf16[128,768]{1,0:T(8,128)(2,1)S(1)}, u32[]{:S(2)}, u32[]{:S(2)}) %collective-permute-start.3) | collective-permute-done | bytes 196640 | tf_op jit(solution)/shard_map/ppermute | solution.py:378
  9.4 1.0 %copy-done.1 = bf16[128,1152]{1,0:T(8,128)(2,1)S(1)} copy-done((bf16[128,1152]{1,0:T(8,128)(2,1)S(1)}, bf16[128,1152]{1,0:T(8,128)(2,1)}, u32[]{:S(2)}) %copy-start.1) | copy-done | bytes 294936
  10.3 0.5 shard_map.114.refs_5_
  10.9 3.4 %collective-permute-start.4 = (bf16[256,256]{1,0:T(8,128)(2,1)S(1)}, bf16[256,256]{1,0:T(8,128)(2,1)S(1)}, u32[]{:S(2)}, u32[]{:S(2)}) collective-permute-start(bf16[256,256]{1,0:T(8,128)(2,1)S(1)} %shard_map.114.refs_5_), channel_id=1, source_target_pairs={{0,128},{4,132},{8,136},{12,140},{16,144},{20,148},{24,152},{28,15... | collective-permute-start | bytes 393224 | tf_op jit(solution)/shard_map/ppermute | solution.py:382
  14.2 1.6 %collective-permute-start = (bf16[128,1152]{1,0:T(8,128)(2,1)}, bf16[128,1152]{1,0:T(8,128)(2,1)S(1)}, u32[]{:S(2)}, u32[]{:S(2)}) collective-permute-start(bf16[128,1152]{1,0:T(8,128)(2,1)} %get-tuple-element.39), channel_id=1, source_target_pairs={{0,4},{4,8},{8,12},{12,0},{16,20},{20,24},{24,28},{28,16},{32,36},... | collective-permute-start | bytes 884744 | tf_op jit(solution)/shard_map/ppermute | solution.py:370
  15.8 0.9 %collective-permute-start.1 = (bf16[128,1152]{1,0:T(8,128)(2,1)}, bf16[128,1152]{1,0:T(8,128)(2,1)S(1)}, u32[]{:S(2)}, u32[]{:S(2)}) collective-permute-start(bf16[128,1152]{1,0:T(8,128)(2,1)} %get-tuple-element.40), channel_id=1, source_target_pairs={{0,8},{4,12},{8,0},{12,4},{16,24},{20,28},{24,16},{28,20},{32,40},... | collective-permute-start | bytes 884744 | tf_op jit(solution)/shard_map/ppermute | solution.py:370
  16.7 2.4 %collective-permute-start.2 = (bf16[128,1152]{1,0:T(8,128)(2,1)}, bf16[128,1152]{1,0:T(8,128)(2,1)S(1)}, u32[]{:S(2)}, u32[]{:S(2)}) collective-permute-start(bf16[128,1152]{1,0:T(8,128)(2,1)} %get-tuple-element.41), channel_id=1, source_target_pairs={{0,12},{4,0},{8,4},{12,8},{16,28},{20,16},{24,20},{28,24},{32,44},... | collective-permute-start | bytes 884744 | tf_op jit(solution)/shard_map/ppermute | solution.py:370
  19.2 1.9 %collective-permute-start.9 = (bf16[256,256]{1,0:T(8,128)(2,1)S(1)}, bf16[256,256]{1,0:T(8,128)(2,1)S(1)}, u32[]{:S(2)}, u32[]{:S(2)}) collective-permute-start(bf16[256,256]{1,0:T(8,128)(2,1)S(1)} %shard_map.114.refs_5_), channel_id=1, source_target_pairs={{0,64},{4,68},{8,72},{12,76},{16,80},{20,84},{24,88},{28,92},{32,9... | collective-permute-start | bytes 393224 | tf_op jit(solution)/shard_map/ppermute | solution.py:382
  21.3 0.8 shard_map.115.refs_6_.refs_5_
  22.1 4.1 %collective-permute-done.9.refs_6_ = bf16[256,256]{1,0:T(8,128)(2,1)S(1)} collective-permute-done((bf16[256,256]{1,0:T(8,128)(2,1)S(1)}, bf16[256,256]{1,0:T(8,128)(2,1)S(1)}, u32[]{:S(2)}, u32[]{:S(2)}) %collective-permute-start.9) | collective-permute-done | bytes 131104 | tf_op jit(solution)/shard_map/ppermute | solution.py:382
  26.2 2.8 %collective-permute-start.11 = (bf16[128,512]{1,0:T(8,128)(2,1)S(1)}, bf16[128,512]{1,0:T(8,128)(2,1)S(1)}, u32[]{:S(2)}, u32[]{:S(2)}) collective-permute-start(bf16[128,512]{1,0:T(8,128)(2,1)S(1)} %get-tuple-element.75), channel_id=1, source_target_pairs={{0,48},{4,52},{8,56},{12,60},{16,32},{20,36},{24,40},{28,44},{32,1... | collective-permute-start | bytes 393224 | tf_op jit(solution)/shard_map/ppermute | solution.py:378
  29.0 1.9 %collective-permute-start.10 = (bf16[128,512]{1,0:T(8,128)(2,1)S(1)}, bf16[128,512]{1,0:T(8,128)(2,1)S(1)}, u32[]{:S(2)}, u32[]{:S(2)}) collective-permute-start(bf16[128,512]{1,0:T(8,128)(2,1)S(1)} %get-tuple-element.74.refs_1_), channel_id=1, source_target_pairs={{0,32},{4,36},{8,40},{12,44},{16,48},{20,52},{24,56},{28,60},{32,0... | collective-permute-start | bytes 393224 | tf_op jit(solution)/shard_map/ppermute | solution.py:378
  30.9 1.6 %collective-permute-start.18 = (bf16[1024,256]{1,0:T(8,128)(2,1)S(1)}, bf16[1024,256]{1,0:T(8,128)(2,1)S(1)}, u32[]{:S(2)}, u32[]{:S(2)}) collective-permute-start(bf16[1024,256]{1,0:T(8,128)(2,1)S(1)} %pad_maximum_fusion.refs_5_), channel_id=1, source_target_pairs={{0,4},{4,8},{8,12},{12,0},{16,20},{20,24},{24,28},{28,16},{32,36},... | collective-permute-start | bytes 1572872 | tf_op jit(solution)/shard_map/ppermute | solution.py:370
  32.6 0.5 collective-permute-start.22
  33.0 1.7 %shard_map.116 = (bf16[272,128]{1,0:T(8,128)(2,1)S(1)}, bf16[272,128]{1,0:T(8,128)(2,1)S(1)}, bf16[272,128]{1,0:T(8,128)(2,1)S(1)}, bf16[272,128]{1,0:T(8,128)(2...) custom-call(s32[4]{0:T(128)S(1)} %pad_add_fusion.refs_0_.place, ...), custom_call_target="tpu_custom_call" | custom-call | flops 629145600 | bytes 2097152 | tf_op jit(solution)/shard_map/pallas_call | solution.py:42
  34.8 0.7 collective-permute-start.6
  35.5 2.3 %collective-permute-start.7 = (bf16[272,128]{1,0:T(8,128)(2,1)S(1)}, bf16[272,128]{1,0:T(8,128)(2,1)S(1)}, u32[]{:S(2)}, u32[]{:S(2)}) collective-permute-start(bf16[272,128]{1,0:T(8,128)(2,1)S(1)} %get-tuple-element.47), channel_id=1, source_target_pairs={{0,32},{4,36},{8,40},{12,44},{16,48},{20,52},{24,56},{28,60},{32,0... | collective-permute-start | bytes 208904 | tf_op jit(solution)/shard_map/ppermute | solution.py:374
  37.7 1.4 %collective-permute-start.8 = (bf16[272,128]{1,0:T(8,128)(2,1)S(1)}, bf16[272,128]{1,0:T(8,128)(2,1)S(1)}, u32[]{:S(2)}, u32[]{:S(2)}) collective-permute-start(bf16[272,128]{1,0:T(8,128)(2,1)S(1)} %get-tuple-element.48), channel_id=1, source_target_pairs={{0,48},{4,52},{8,56},{12,60},{16,0},{20,4},{24,8},{28,12},{32,16},... | collective-permute-start | bytes 208904 | tf_op jit(solution)/shard_map/ppermute | solution.py:374
  39.1 3.7 %shard_map.117 = (f32[2048,128]{1,0:T(8,128)S(1)}, f32[2048,128]{1,0:T(8,128)S(1)}, f32[2048,128]{1,0:T(8,128)S(1)}) custom-call(s32[4]{0:T(128)S(1)} %pad_add_fusion.refs_0_.place, bf16[128,512]{1,0:T(8,128)(2,1)S(1)} %get-tuple-element.74.refs_1_, bf16[128,768]{1,0:T(8,128)(2,1)S(1)} %collective-permute-done.3.refs_2_, ...), custom_call_target="tpu_custom_call" | custom-call | flops 4294967296 | bytes 8388608 | tf_op jit(solution)/shard_map/pallas_call | solution.py:42
  42.9 0.7 shard_map.118
  43.6 3.5 %collective-permute-start.12 = (bf16[272,128]{1,0:T(8,128)(2,1)S(1)}, bf16[272,128]{1,0:T(8,128)(2,1)S(1)}, u32[]{:S(2)}, u32[]{:S(2)}) collective-permute-start(bf16[272,128]{1,0:T(8,128)(2,1)S(1)} %get-tuple-element.50.refs_5_), channel_id=1, source_target_pairs={{0,64},{4,68},{8,72},{12,76},{16,80},{20,84},{24,88},{28,92},{32,9... | collective-permute-start | bytes 208904 | tf_op jit(solution)/shard_map/ppermute | solution.py:382
  47.1 2.5 %collective-permute-start.14 = (bf16[272,128]{1,0:T(8,128)(2,1)S(1)}, bf16[272,128]{1,0:T(8,128)(2,1)S(1)}, u32[]{:S(2)}, u32[]{:S(2)}) collective-permute-start(bf16[272,128]{1,0:T(8,128)(2,1)S(1)} %get-tuple-element.50.refs_5_), channel_id=1, source_target_pairs={{0,192},{4,196},{8,200},{12,204},{16,208},{20,212},{24,216},{28,22... | collective-permute-start | bytes 208904 | tf_op jit(solution)/shard_map/ppermute | solution.py:382
  49.5 2.1 %shard_map.119 = (f32[4,128,512]{2,1,0:T(8,128)S(1)}, f32[4,128,512]{2,1,0:T(8,128)S(1)}) custom-call(s32[4]{0:T(128)S(1)} %pad_add_fusion.refs_0_.place, bf16[4,128,1152]{2,1,0:T(8,128)(2,1)S(1)} %get-tuple-element.42.refs_1_, f32[4,128,512]{2,1,0:T(8,128)S(1)} %get-tuple-element.43.refs_2_, f32[4,256,512]{2,1,0:T(8,128)S(1)} %get-tuple-element.44.refs_3_, ...), custom_call_target="tpu_custom_call" | custom-call | flops 2147483648 | bytes 4194304 | tf_op jit(solution)/shard_map/pallas_call | solution.py:42
  51.8 0.8 collective-permute-done.13.refs_6_
  52.6 0.7 shard_map.120
  53.4 3.2 %collective-permute-start.16 = (bf16[256,128]{1,0:T(8,128)(2,1)S(1)}, bf16[256,128]{1,0:T(8,128)(2,1)S(1)}, u32[]{:S(2)}, u32[]{:S(2)}) collective-permute-start(bf16[256,128]{1,0:T(8,128)(2,1)S(1)} %get-tuple-element.55), channel_id=1, source_target_pairs={{0,32},{4,36},{8,40},{12,44},{16,48},{20,52},{24,56},{28,60},{32,0... | collective-permute-start | bytes 196616 | tf_op jit(solution)/shard_map/ppermute | solution.py:374
  56.6 0.1 collective-permute-start.17
  56.7 4.0 %shard_map.121 = (f32[2048,128]{1,0:T(8,128)S(1)}, f32[2048,128]{1,0:T(8,128)S(1)}, f32[2048,128]{1,0:T(8,128)S(1)}) custom-call(s32[4]{0:T(128)S(1)} %pad_add_fusion.refs_0_.place, bf16[128,512]{1,0:T(8,128)(2,1)S(1)} %get-tuple-element.74.refs_1_, ...), custom_call_target="tpu_custom_call", output_to_operand_aliasing={{0}: (5, {}), {1}: (6, {}), {2}: (7, {})} | custom-call | flops 4294967296 | bytes 8388608 | tf_op jit(solution)/shard_map/pallas_call | solution.py:42
  60.7 0.1 collective-permute-done.17.refs_7_
  60.8 1.0 %shard_map.122 = (bf16[128,512]{1,0:T(8,128)(2,1)S(1)}, bf16[128,512]{1,0:T(8,128)(2,1)S(1)}, bf16[128,512]{1,0:T(8,128)(2,1)S(1)}, bf16[128,512]{1,0:T(8,128)(2,1)S(1)}) custom-call(s32[4]{0:T(128)S(1)} %pad_add_fusion.refs_0_.place, bf16[4,128,1152]{2,1,0:T(8,128)(2,1)S(1)} %get-tuple-element.42.refs_1_, ...), custom_call_target="tpu_custom_call" | custom-call | flops 1000000 | bytes 1000000 | tf_op jit(solution)/shard_map/pallas_call | solution.py:42
  61.8 2.3 %collective-permute-start.19 = (bf16[128,512]{1,0:T(8,128)(2,1)S(1)}, bf16[128,512]{1,0:T(8,128)(2,1)S(1)}, u32[]{:S(2)}, u32[]{:S(2)}) collective-permute-start(bf16[128,512]{1,0:T(8,128)(2,1)S(1)} %get-tuple-element.61), channel_id=1, source_target_pairs={{0,4},{4,8},{8,12},{12,0},{16,20},{20,24},{24,28},{28,16},{32,36},... | collective-permute-start | bytes 393224 | tf_op jit(solution)/shard_map/ppermute | solution.py:370
  64.2 1.8 %collective-permute-start.20 = (bf16[128,512]{1,0:T(8,128)(2,1)S(1)}, bf16[128,512]{1,0:T(8,128)(2,1)S(1)}, u32[]{:S(2)}, u32[]{:S(2)}) collective-permute-start(bf16[128,512]{1,0:T(8,128)(2,1)S(1)} %get-tuple-element.62), channel_id=1, source_target_pairs={{0,8},{4,12},{8,0},{12,4},{16,24},{20,28},{24,16},{28,20},{32,40},... | collective-permute-start | bytes 393224 | tf_op jit(solution)/shard_map/ppermute | solution.py:370
  65.9 1.3 %collective-permute-start.21 = (bf16[128,512]{1,0:T(8,128)(2,1)S(1)}, bf16[128,512]{1,0:T(8,128)(2,1)S(1)}, u32[]{:S(2)}, u32[]{:S(2)}) collective-permute-start(bf16[128,512]{1,0:T(8,128)(2,1)S(1)} %get-tuple-element.63), channel_id=1, source_target_pairs={{0,12},{4,0},{8,4},{12,8},{16,28},{20,16},{24,20},{28,24},{32,44},... | collective-permute-start | bytes 393224 | tf_op jit(solution)/shard_map/ppermute | solution.py:370
  67.2 3.8 %shard_map.123 = (f32[2048,128]{1,0:T(8,128)S(1)}, f32[2048,128]{1,0:T(8,128)S(1)}, f32[2048,128]{1,0:T(8,128)S(1)}) custom-call(s32[4]{0:T(128)S(1)} %pad_add_fusion.refs_0_.place, bf16[128,512]{1,0:T(8,128)(2,1)S(1)} %get-tuple-element.74.refs_1_, ...), custom_call_target="tpu_custom_call", output_to_operand_aliasing={{0}: (5, {}), {1}: (6, {}), {2}: (7, {})} | custom-call | flops 4294967296 | bytes 8388608 | tf_op jit(solution)/shard_map/pallas_call | solution.py:42
  71.0 1.0 %collective-permute-done.21.refs_11_.refs_4_ = bf16[128,512]{1,0:T(8,128)(2,1)S(1)} collective-permute-done((bf16[128,512]{1,0:T(8,128)(2,1)S(1)}, bf16[128,512]{1,0:T(8,128)(2,1)S(1)}, u32[]{:S(2)}, u32[]{:S(2)}) %collective-permute-start.21) | collective-permute-done | bytes 131104 | tf_op jit(solution)/shard_map/ppermute | solution.py:370
  72.0 4.1 %shard_map.124 = (f32[2048,128]{1,0:T(8,128)S(1)}, f32[2048,128]{1,0:T(8,128)S(1)}, f32[2048,128]{1,0:T(8,128)S(1)}, bf16[128,640]{1,0:T(8,128)(2,1)S(1)}, bf16[...) custom-call(s32[4]{0:T(128)S(1)} %pad_add_fusion.refs_0_.place, ...), custom_call_target="tpu_custom_call", output_to_operand_aliasing={{0}: (5, {}), {1}: (6, {}), {2}: (7, {})} | custom-call | flops 4294967296 | bytes 8388608 | tf_op jit(solution)/shard_map/pallas_call | solution.py:42
  76.1 0.9 %collective-permute-start.24 = (bf16[128,640]{1,0:T(8,128)(2,1)S(1)}, bf16[128,640]{1,0:T(8,128)(2,1)S(1)}, u32[]{:S(2)}, u32[]{:S(2)}) collective-permute-start(bf16[128,640]{1,0:T(8,128)(2,1)S(1)} %get-tuple-element.71), channel_id=1, source_target_pairs={{0,16},{4,20},{8,24},{12,28},{16,0},{20,4},{24,8},{28,12},{32,48},... | collective-permute-start | bytes 491528 | tf_op jit(solution)/shard_map/ppermute | solution.py:378
  77.1 2.1 %collective-permute-start.25 = (bf16[128,640]{1,0:T(8,128)(2,1)S(1)}, bf16[128,640]{1,0:T(8,128)(2,1)S(1)}, u32[]{:S(2)}, u32[]{:S(2)}) collective-permute-start(bf16[128,640]{1,0:T(8,128)(2,1)S(1)} %get-tuple-element.72), channel_id=1, source_target_pairs={{0,32},{4,36},{8,40},{12,44},{16,48},{20,52},{24,56},{28,60},{32,0... | collective-permute-start | bytes 491528 | tf_op jit(solution)/shard_map/ppermute | solution.py:378
  79.2 1.8 %collective-permute-start.26 = (bf16[128,640]{1,0:T(8,128)(2,1)S(1)}, bf16[128,640]{1,0:T(8,128)(2,1)S(1)}, u32[]{:S(2)}, u32[]{:S(2)}) collective-permute-start(bf16[128,640]{1,0:T(8,128)(2,1)S(1)} %get-tuple-element.73), channel_id=1, source_target_pairs={{0,48},{4,52},{8,56},{12,60},{16,32},{20,36},{24,40},{28,44},{32,1... | collective-permute-start | bytes 491528 | tf_op jit(solution)/shard_map/ppermute | solution.py:378
  80.9 1.7 %shard_map.125 = bf16[128,2048]{1,0:T(8,128)(2,1)} custom-call(s32[4]{0:T(128)S(1)} %pad_add_fusion.refs_0_.place, bf16[128,512]{1,0:T(8,128)(2,1)S(1)} %get-tuple-element.60.refs_9_.refs_1_, bf16[128,512]{1,0:T(8,128)(2,1)S(1)} %collective-permute-done.19.refs_9_.refs_2_, bf16[128,512]{1,0:T(8,128)(2,1)S(1)} %collective-permute-done.20.refs_10_.refs_3_, ...), custom_call_target="tpu_custom_call" | custom-call | flops 1000000 | bytes 1000000 | tf_op jit(solution)/shard_map/pallas_call | solution.py:42
  82.6 1.7 %collective-permute-done.25.o2 = bf16[128,640]{1,0:T(8,128)(2,1)S(1)} collective-permute-done((bf16[128,640]{1,0:T(8,128)(2,1)S(1)}, bf16[128,640]{1,0:T(8,128)(2,1)S(1)}, u32[]{:S(2)}, u32[]{:S(2)}) %collective-permute-start.25) | collective-permute-done | bytes 163872 | tf_op jit(solution)/shard_map/ppermute | solution.py:378
  84.2 1.7 %collective-permute-done.26.o3 = bf16[128,640]{1,0:T(8,128)(2,1)S(1)} collective-permute-done((bf16[128,640]{1,0:T(8,128)(2,1)S(1)}, bf16[128,640]{1,0:T(8,128)(2,1)S(1)}, u32[]{:S(2)}, u32[]{:S(2)}) %collective-permute-start.26) | collective-permute-done | bytes 163872 | tf_op jit(solution)/shard_map/ppermute | solution.py:378
  86.0 2.1 %shard_map.126 = bf16[128,1024]{1,0:T(8,128)(2,1)} custom-call(s32[4]{0:T(128)S(1)} %pad_add_fusion.refs_0_.place, bf16[128,640]{1,0:T(8,128)(2,1)S(1)} %get-tuple-element.70.refs_7_.o0, bf16[128,640]{1,0:T(8,128)(2,1)S(1)} %collective-permute-done.24.o1, bf16[128,640]{1,0:T(8,128)(2,1)S(1)} %collective-permute-done.25.o2, ...), custom_call_target="tpu_custom_call" | custom-call | flops 1000000 | bytes 1000000 | tf_op jit(solution)/shard_map/pallas_call | solution.py:42
  (43 shorter events, 0.7 us)
Async XLA Ops:
  0.6 3.6 %copy-start = (f32[128,32]{0,1:T(8,128)S(1)}, f32[128,32]{0,1:T(8,128)}, u32[]{:S(2)}) copy-start(f32[128,32]{0,1:T(8,128)} %param.11) | copy-start | bytes 49156
  0.6 20.5 %copy-start.5 = (f32[32]{0:T(128)S(1)}, f32[32]{0:T(128)}, u32[]{:S(2)}) copy-start(f32[32]{0:T(128)} %param.15) | copy-start | bytes 388
  0.7 20.6 %copy-start.3 = (bf16[128,2048]{1,0:T(8,128)(2,1)S(1)}, bf16[128,2048]{1,0:T(8,128)(2,1)}, u32[]{:S(2)}) copy-start(bf16[128,2048]{1,0:T(8,128)(2,1)} %gate.1) | copy-start | bytes 1572868
  2.6 6.7 %collective-permute-start.3 = (bf16[128,768]{1,0:T(8,128)(2,1)S(1)}, bf16[128,768]{1,0:T(8,128)(2,1)S(1)}, u32[]{:S(2)}, u32[]{:S(2)}) collective-permute-start(bf16[128,768]{1,0:T(8,128)(2,1)S(1)} %pad_maximum_fusion.1), channel_id=1, source_target_pairs={{0,16},{4,20},{8,24},{12,28},{16,0},{20,4},{24,8},{28,12},{32,48},... | collective-permute-start | bytes 589832 | tf_op jit(solution)/shard_map/ppermute | solution.py:378
  9.3 1.0 %copy-start.1 = (bf16[128,1152]{1,0:T(8,128)(2,1)S(1)}, bf16[128,1152]{1,0:T(8,128)(2,1)}, u32[]{:S(2)}) copy-start(bf16[128,1152]{1,0:T(8,128)(2,1)} %get-tuple-element.38.refs_3_.refs_1_) | copy-start | bytes 884740
  10.3 22.7 %copy-start.2 = (bf16[128,1152]{1,0:T(8,128)(2,1)S(1)}, bf16[128,1152]{1,0:T(8,128)(2,1)}, u32[]{:S(2)}) copy-start(bf16[128,1152]{1,0:T(8,128)(2,1)} %get-tuple-element.38.refs_3_.refs_1_) | copy-start | bytes 884740
  10.9 10.2 %collective-permute-start.4 = (bf16[256,256]{1,0:T(8,128)(2,1)S(1)}, bf16[256,256]{1,0:T(8,128)(2,1)S(1)}, u32[]{:S(2)}, u32[]{:S(2)}) collective-permute-start(bf16[256,256]{1,0:T(8,128)(2,1)S(1)} %shard_map.114.refs_5_), channel_id=1, source_target_pairs={{0,128},{4,132},{8,136},{12,140},{16,144},{20,148},{24,152},{28,15... | collective-permute-start | bytes 393224 | tf_op jit(solution)/shard_map/ppermute | solution.py:382
  14.2 16.7 %collective-permute-start = (bf16[128,1152]{1,0:T(8,128)(2,1)}, bf16[128,1152]{1,0:T(8,128)(2,1)S(1)}, u32[]{:S(2)}, u32[]{:S(2)}) collective-permute-start(bf16[128,1152]{1,0:T(8,128)(2,1)} %get-tuple-element.39), channel_id=1, source_target_pairs={{0,4},{4,8},{8,12},{12,0},{16,20},{20,24},{24,28},{28,16},{32,36},... | collective-permute-start | bytes 884744 | tf_op jit(solution)/shard_map/ppermute | solution.py:370
  15.8 16.8 %collective-permute-start.1 = (bf16[128,1152]{1,0:T(8,128)(2,1)}, bf16[128,1152]{1,0:T(8,128)(2,1)S(1)}, u32[]{:S(2)}, u32[]{:S(2)}) collective-permute-start(bf16[128,1152]{1,0:T(8,128)(2,1)} %get-tuple-element.40), channel_id=1, source_target_pairs={{0,8},{4,12},{8,0},{12,4},{16,24},{20,28},{24,16},{28,20},{32,40},... | collective-permute-start | bytes 884744 | tf_op jit(solution)/shard_map/ppermute | solution.py:370
  16.7 16.3 %collective-permute-start.2 = (bf16[128,1152]{1,0:T(8,128)(2,1)}, bf16[128,1152]{1,0:T(8,128)(2,1)S(1)}, u32[]{:S(2)}, u32[]{:S(2)}) collective-permute-start(bf16[128,1152]{1,0:T(8,128)(2,1)} %get-tuple-element.41), channel_id=1, source_target_pairs={{0,12},{4,0},{8,4},{12,8},{16,28},{20,16},{24,20},{28,24},{32,44},... | collective-permute-start | bytes 884744 | tf_op jit(solution)/shard_map/ppermute | solution.py:370
  19.2 7.1 %collective-permute-start.9 = (bf16[256,256]{1,0:T(8,128)(2,1)S(1)}, bf16[256,256]{1,0:T(8,128)(2,1)S(1)}, u32[]{:S(2)}, u32[]{:S(2)}) collective-permute-start(bf16[256,256]{1,0:T(8,128)(2,1)S(1)} %shard_map.114.refs_5_), channel_id=1, source_target_pairs={{0,64},{4,68},{8,72},{12,76},{16,80},{20,84},{24,88},{28,92},{32,9... | collective-permute-start | bytes 393224 | tf_op jit(solution)/shard_map/ppermute | solution.py:382
  21.1 7.9 %collective-permute-start.5 = (bf16[256,256]{1,0:T(8,128)(2,1)S(1)}, bf16[256,256]{1,0:T(8,128)(2,1)S(1)}, u32[]{:S(2)}, u32[]{:S(2)}) collective-permute-start(bf16[256,256]{1,0:T(8,128)(2,1)S(1)} %collective-permute-done.4.refs_7_), channel_id=1, source_target_pairs={{0,64},{4,68},{8,72},{12,76},{16,80},{20,84},{24,88},{28,92},{32,9... | collective-permute-start | bytes 393224 | tf_op jit(solution)/shard_map/ppermute | solution.py:382
  26.2 11.5 %collective-permute-start.11 = (bf16[128,512]{1,0:T(8,128)(2,1)S(1)}, bf16[128,512]{1,0:T(8,128)(2,1)S(1)}, u32[]{:S(2)}, u32[]{:S(2)}) collective-permute-start(bf16[128,512]{1,0:T(8,128)(2,1)S(1)} %get-tuple-element.75), channel_id=1, source_target_pairs={{0,48},{4,52},{8,56},{12,60},{16,32},{20,36},{24,40},{28,44},{32,1... | collective-permute-start | bytes 393224 | tf_op jit(solution)/shard_map/ppermute | solution.py:378
  29.0 6.5 %collective-permute-start.10 = (bf16[128,512]{1,0:T(8,128)(2,1)S(1)}, bf16[128,512]{1,0:T(8,128)(2,1)S(1)}, u32[]{:S(2)}, u32[]{:S(2)}) collective-permute-start(bf16[128,512]{1,0:T(8,128)(2,1)S(1)} %get-tuple-element.74.refs_1_), channel_id=1, source_target_pairs={{0,32},{4,36},{8,40},{12,44},{16,48},{20,52},{24,56},{28,60},{32,0... | collective-permute-start | bytes 393224 | tf_op jit(solution)/shard_map/ppermute | solution.py:378
  30.9 25.6 %collective-permute-start.18 = (bf16[1024,256]{1,0:T(8,128)(2,1)S(1)}, bf16[1024,256]{1,0:T(8,128)(2,1)S(1)}, u32[]{:S(2)}, u32[]{:S(2)}) collective-permute-start(bf16[1024,256]{1,0:T(8,128)(2,1)S(1)} %pad_maximum_fusion.refs_5_), channel_id=1, source_target_pairs={{0,4},{4,8},{8,12},{12,0},{16,20},{20,24},{24,28},{28,16},{32,36},... | collective-permute-start | bytes 1572872 | tf_op jit(solution)/shard_map/ppermute | solution.py:370
  32.6 34.7 %collective-permute-start.22 = (bf16[1024,256]{1,0:T(8,128)(2,1)S(1)}, bf16[1024,256]{1,0:T(8,128)(2,1)S(1)}, u32[]{:S(2)}, u32[]{:S(2)}) collective-permute-start(bf16[1024,256]{1,0:T(8,128)(2,1)S(1)} %pad_maximum_fusion.refs_5_), channel_id=1, source_target_pairs={{0,12},{4,0},{8,4},{12,8},{16,28},{20,16},{24,20},{28,24},{32,44},... | collective-permute-start | bytes 1572872 | tf_op jit(solution)/shard_map/ppermute | solution.py:370
  34.8 8.1 %collective-permute-start.6 = (bf16[272,128]{1,0:T(8,128)(2,1)S(1)}, bf16[272,128]{1,0:T(8,128)(2,1)S(1)}, u32[]{:S(2)}, u32[]{:S(2)}) collective-permute-start(bf16[272,128]{1,0:T(8,128)(2,1)S(1)} %get-tuple-element.46), channel_id=1, source_target_pairs={{0,16},{4,20},{8,24},{12,28},{16,32},{20,36},{24,40},{28,44},{32,4... | collective-permute-start | bytes 208904 | tf_op jit(solution)/shard_map/ppermute | solution.py:374
  35.5 7.4 %collective-permute-start.7 = (bf16[272,128]{1,0:T(8,128)(2,1)S(1)}, bf16[272,128]{1,0:T(8,128)(2,1)S(1)}, u32[]{:S(2)}, u32[]{:S(2)}) collective-permute-start(bf16[272,128]{1,0:T(8,128)(2,1)S(1)} %get-tuple-element.47), channel_id=1, source_target_pairs={{0,32},{4,36},{8,40},{12,44},{16,48},{20,52},{24,56},{28,60},{32,0... | collective-permute-start | bytes 208904 | tf_op jit(solution)/shard_map/ppermute | solution.py:374
  37.7 5.2 %collective-permute-start.8 = (bf16[272,128]{1,0:T(8,128)(2,1)S(1)}, bf16[272,128]{1,0:T(8,128)(2,1)S(1)}, u32[]{:S(2)}, u32[]{:S(2)}) collective-permute-start(bf16[272,128]{1,0:T(8,128)(2,1)S(1)} %get-tuple-element.48), channel_id=1, source_target_pairs={{0,48},{4,52},{8,56},{12,60},{16,0},{20,4},{24,8},{28,12},{32,16},... | collective-permute-start | bytes 208904 | tf_op jit(solution)/shard_map/ppermute | solution.py:374
  43.6 8.1 %collective-permute-start.12 = (bf16[272,128]{1,0:T(8,128)(2,1)S(1)}, bf16[272,128]{1,0:T(8,128)(2,1)S(1)}, u32[]{:S(2)}, u32[]{:S(2)}) collective-permute-start(bf16[272,128]{1,0:T(8,128)(2,1)S(1)} %get-tuple-element.50.refs_5_), channel_id=1, source_target_pairs={{0,64},{4,68},{8,72},{12,76},{16,80},{20,84},{24,88},{28,92},{32,9... | collective-permute-start | bytes 208904 | tf_op jit(solution)/shard_map/ppermute | solution.py:382
  47.1 5.5 %collective-permute-start.13 = (bf16[272,128]{1,0:T(8,128)(2,1)S(1)}, bf16[272,128]{1,0:T(8,128)(2,1)S(1)}, u32[]{:S(2)}, u32[]{:S(2)}) collective-permute-start(bf16[272,128]{1,0:T(8,128)(2,1)S(1)} %get-tuple-element.50.refs_5_), channel_id=1, source_target_pairs={{0,128},{4,132},{8,136},{12,140},{16,144},{20,148},{24,152},{28,15... | collective-permute-start | bytes 208904 | tf_op jit(solution)/shard_map/ppermute | solution.py:382
  47.1 5.5 %collective-permute-start.14 = (bf16[272,128]{1,0:T(8,128)(2,1)S(1)}, bf16[272,128]{1,0:T(8,128)(2,1)S(1)}, u32[]{:S(2)}, u32[]{:S(2)}) collective-permute-start(bf16[272,128]{1,0:T(8,128)(2,1)S(1)} %get-tuple-element.50.refs_5_), channel_id=1, source_target_pairs={{0,192},{4,196},{8,200},{12,204},{16,208},{20,212},{24,216},{28,22... | collective-permute-start | bytes 208904 | tf_op jit(solution)/shard_map/ppermute | solution.py:382
  51.7 19.4 %collective-permute-start.23 = (bf16[1024,256]{1,0:T(8,128)(2,1)S(1)}, bf16[1024,256]{1,0:T(8,128)(2,1)S(1)}, u32[]{:S(2)}, u32[]{:S(2)}) collective-permute-start(bf16[1024,256]{1,0:T(8,128)(2,1)S(1)} %get-tuple-element.69), channel_id=1, source_target_pairs={{0,8},{4,12},{8,0},{12,4},{16,24},{20,28},{24,16},{28,20},{32,40},... | collective-permute-start | bytes 1572872 | tf_op jit(solution)/shard_map/ppermute | solution.py:370
  53.3 7.4 %collective-permute-start.15 = (bf16[256,128]{1,0:T(8,128)(2,1)S(1)}, bf16[256,128]{1,0:T(8,128)(2,1)S(1)}, u32[]{:S(2)}, u32[]{:S(2)}) collective-permute-start(bf16[256,128]{1,0:T(8,128)(2,1)S(1)} %get-tuple-element.54), channel_id=1, source_target_pairs={{0,16},{4,20},{8,24},{12,28},{16,32},{20,36},{24,40},{28,44},{32,4... | collective-permute-start | bytes 196616 | tf_op jit(solution)/shard_map/ppermute | solution.py:374
  53.4 7.3 %collective-permute-start.16 = (bf16[256,128]{1,0:T(8,128)(2,1)S(1)}, bf16[256,128]{1,0:T(8,128)(2,1)S(1)}, u32[]{:S(2)}, u32[]{:S(2)}) collective-permute-start(bf16[256,128]{1,0:T(8,128)(2,1)S(1)} %get-tuple-element.55), channel_id=1, source_target_pairs={{0,32},{4,36},{8,40},{12,44},{16,48},{20,52},{24,56},{28,60},{32,0... | collective-permute-start | bytes 196616 | tf_op jit(solution)/shard_map/ppermute | solution.py:374
  56.6 4.3 %collective-permute-start.17 = (bf16[256,128]{1,0:T(8,128)(2,1)S(1)}, bf16[256,128]{1,0:T(8,128)(2,1)S(1)}, u32[]{:S(2)}, u32[]{:S(2)}) collective-permute-start(bf16[256,128]{1,0:T(8,128)(2,1)S(1)} %get-tuple-element.56), channel_id=1, source_target_pairs={{0,48},{4,52},{8,56},{12,60},{16,0},{20,4},{24,8},{28,12},{32,16},... | collective-permute-start | bytes 196616 | tf_op jit(solution)/shard_map/ppermute | solution.py:374
  61.8 9.2 %collective-permute-start.19 = (bf16[128,512]{1,0:T(8,128)(2,1)S(1)}, bf16[128,512]{1,0:T(8,128)(2,1)S(1)}, u32[]{:S(2)}, u32[]{:S(2)}) collective-permute-start(bf16[128,512]{1,0:T(8,128)(2,1)S(1)} %get-tuple-element.61), channel_id=1, source_target_pairs={{0,4},{4,8},{8,12},{12,0},{16,20},{20,24},{24,28},{28,16},{32,36},... | collective-permute-start | bytes 393224 | tf_op jit(solution)/shard_map/ppermute | solution.py:370
  64.2 6.9 %collective-permute-start.20 = (bf16[128,512]{1,0:T(8,128)(2,1)S(1)}, bf16[128,512]{1,0:T(8,128)(2,1)S(1)}, u32[]{:S(2)}, u32[]{:S(2)}) collective-permute-start(bf16[128,512]{1,0:T(8,128)(2,1)S(1)} %get-tuple-element.62), channel_id=1, source_target_pairs={{0,8},{4,12},{8,0},{12,4},{16,24},{20,28},{24,16},{28,20},{32,40},... | collective-permute-start | bytes 393224 | tf_op jit(solution)/shard_map/ppermute | solution.py:370
  65.9 6.1 %collective-permute-start.21 = (bf16[128,512]{1,0:T(8,128)(2,1)S(1)}, bf16[128,512]{1,0:T(8,128)(2,1)S(1)}, u32[]{:S(2)}, u32[]{:S(2)}) collective-permute-start(bf16[128,512]{1,0:T(8,128)(2,1)S(1)} %get-tuple-element.63), channel_id=1, source_target_pairs={{0,12},{4,0},{8,4},{12,8},{16,28},{20,16},{24,20},{28,24},{32,44},... | collective-permute-start | bytes 393224 | tf_op jit(solution)/shard_map/ppermute | solution.py:370
  72.0 8.9 %copy-start.4 = (f32[2048]{0:T(1024)S(1)}, f32[2048]{0:T(1024)}, u32[]{:S(2)}) copy-start(f32[2048]{0:T(1024)} %param.16) | copy-start | bytes 24580
  76.1 6.4 %collective-permute-start.24 = (bf16[128,640]{1,0:T(8,128)(2,1)S(1)}, bf16[128,640]{1,0:T(8,128)(2,1)S(1)}, u32[]{:S(2)}, u32[]{:S(2)}) collective-permute-start(bf16[128,640]{1,0:T(8,128)(2,1)S(1)} %get-tuple-element.71), channel_id=1, source_target_pairs={{0,16},{4,20},{8,24},{12,28},{16,0},{20,4},{24,8},{28,12},{32,48},... | collective-permute-start | bytes 491528 | tf_op jit(solution)/shard_map/ppermute | solution.py:378
  77.1 7.2 %collective-permute-start.25 = (bf16[128,640]{1,0:T(8,128)(2,1)S(1)}, bf16[128,640]{1,0:T(8,128)(2,1)S(1)}, u32[]{:S(2)}, u32[]{:S(2)}) collective-permute-start(bf16[128,640]{1,0:T(8,128)(2,1)S(1)} %get-tuple-element.72), channel_id=1, source_target_pairs={{0,32},{4,36},{8,40},{12,44},{16,48},{20,52},{24,56},{28,60},{32,0... | collective-permute-start | bytes 491528 | tf_op jit(solution)/shard_map/ppermute | solution.py:378
  79.2 6.8 %collective-permute-start.26 = (bf16[128,640]{1,0:T(8,128)(2,1)S(1)}, bf16[128,640]{1,0:T(8,128)(2,1)S(1)}, u32[]{:S(2)}, u32[]{:S(2)}) collective-permute-start(bf16[128,640]{1,0:T(8,128)(2,1)S(1)} %get-tuple-element.73), channel_id=1, source_target_pairs={{0,48},{4,52},{8,56},{12,60},{16,32},{20,36},{24,40},{28,44},{32,1... | collective-permute-start | bytes 491528 | tf_op jit(solution)/shard_map/ppermute | solution.py:378
where the time goes:
time: 88.3 us; the launch traced here: 88.1 us
  starting transfers between devices  42.6 us (48%)
  Pallas kernels  29.2 us (33%)
  waiting for transfers between devices  11.4 us (13%)
  local copies, waits for them, and re-layouts  3.87 us (4%)
  between operations  0.93 us (1%)
    pallas_call x13, Pallas kernels, run(): pl.pallas_call(body if after else kernel, out_shape=outs, in_specs=[smem]...  26.9 us
    ppermute x9, starting transfers between devices, shift_y(): lax.ppermute(vals, 'ctx', [(i, i & ~3 | i + shift & 3) for i in range(64)])  12.5 us
    ppermute x6, starting transfers between devices, up_z(): lax.ppermute(vals, 'ctx', [(i, i + 16 * shift & 63) for i in range(64)])  11.3 us
    ppermute x6, starting transfers between devices, swap_x(): return lax.ppermute(vals, 'ctx', [(i, i ^ 4 * step) for i in range(64)])  11 us
    ppermute x6, starting transfers between devices, shift_x(): lax.ppermute(vals, 'ctx', [(i, i & ~12 | i + 4 * shift & 12) for i in ran...  7.73 us
    ppermute x6, waiting for transfers between devices, swap_x(): return lax.ppermute(vals, 'ctx', [(i, i ^ 4 * step) for i in range(64)])  5.3 us
    ppermute x6, waiting for transfers between devices, up_z(): lax.ppermute(vals, 'ctx', [(i, i + 16 * shift & 63) for i in range(64)])  4.89 us
    pallas_call x1, Pallas kernels, on_device(): pl.pallas_call(pack_kernel, out_shape=[shape((LBLK, WIDTH), bf16)] * 4, i...  2.31 us
  transfers between devices with their start and end apart: 27, of which 7 were waited for; matrix products, arithmetic and copies ran while one was open for 1% of the time, Pallas kernels for 25%

commit v1 on v0

--- a/solution.py
+++ b/solution.py
@@ -73,15 +73,24 @@
 
 def pack_kernel(decay, x, b, c, *outs):
     y = lax.bitwise_and(lax.axis_index("ctx").astype(jnp.int32), 3)
-    lane = iota((LBLK, 128), 1)
+    head, lane = iota((32, 128), 0), iota((32, 128), 1)
+    parts = split3(decay[...])
     for s, out in enumerate(outs):
         j = ring4(y, s)
         group = lax.shift_right_logical(j, 1)
         out[:, 0:SLICE] = x[:, lanes(j, SLICE)]
         out[:, AT_B:AT_C] = b[:, lanes(group, NSTATE)]
         out[:, AT_C:AT_DECAY] = c[:, lanes(group, NSTATE)]
-        high, mid, low = (part.astype(f32) for part in split3(decay[:, lanes(j, 128)]))
-        out[:, AT_DECAY:] = jnp.where(lane < 8, high, jnp.where(lane < 16, mid, low)).astype(bf16)
+        spread = jnp.zeros((LBLK, 128), f32)
+        for i, part in enumerate(parts):
+            chosen = (head == 8 * j + lax.bitwise_and(lane, 7)) & (lax.shift_right_logical(lane, 3) == i)
+            spread = spread + lax.dot_general(
+                part,
+                jnp.where(chosen, 1.0, 0.0).astype(bf16),
+                (((0,), (0,)), ((), ())),
+                preferred_element_type=f32,
+            )
+        out[:, AT_DECAY:] = spread.astype(bf16)
 
 
 def pair_kernel(place, own, swapped, out):
@@ -285,9 +294,9 @@
     return [score + one for score, one in zip(scores, offsets)]
 
 
-def every_tile(place, queries, keys, values, state, own_plane):
+def every_tile(place, queries, keys, values, state, own_plane, slots=(0, 1, 2, 3)):
     offsets = [offset(place[0] >= distance) for distance in (1, 2, 3)]
-    for tile in range(16):
+    for tile in (slot * 4 + head for slot in slots for head in range(4)):
 
         def limit(scores, slot=tile // 4):
             return [own_plane(scores[0], slot)] + add_offsets(scores[1:], offsets)
@@ -313,7 +322,7 @@
     every_tile(place, (q0, q1, q2, q3), keys, values, (tops, sums, acc), own_plane)
 
 
-def column_attend(step, place, q0, q1, q2, q3, old_tops, old_sums, old_acc, *refs):
+def column_attend(step, slots, place, q0, q1, q2, q3, old_tops, old_sums, old_acc, *refs):
     column, outs = refs[0], refs[1:]
     state = outs[:3]
     x, y = place[1], place[2]
@@ -328,11 +337,11 @@
         near, far = (offset(one * 4 + other < query_block) for one in (x, lax.bitwise_xor(x, 1)))
         return score + jnp.where(lane < LBLK, near, far)
 
-    every_tile(place, (q0, q1, q2, q3), keys, values, state, own_plane)
+    every_tile(place, (q0, q1, q2, q3), keys, values, state, own_plane, slots)
     if step == 2:
         tops, sums, acc = state
         lane = iota((LBLK, 128), 1)
-        for s, o in enumerate(outs[3:]):
+        for s, o in zip(slots, outs[3:]):
             stats = jnp.zeros((LBLK, 128), f32)
             for head in range(4):
                 start = (s * 4 + head) * LBLK
@@ -387,8 +396,6 @@
 ):
     index = lax.axis_index("ctx").astype(jnp.int32)
     place = jnp.stack([index // 16, (index // 4) % 4, index % 4, index])
-    decay_copies = jnp.tile(log_decay.reshape(LBLK, 4, 1, 8), (1, 1, 3, 1)).reshape(LBLK, 4, 24)
-    decay_grid = jnp.pad(decay_copies, ((0, 0), (0, 0), (0, 104))).reshape(LBLK, 512)
     skip = jnp.repeat(skip_gain, MHDIM).reshape(1, 4 * SLICE)
     gain = norm_gain.reshape(1, 4 * SLICE)
 
@@ -410,7 +417,7 @@
         in_specs=[vmem] * 4,
         out_specs=[vmem] * 4,
         compiler_params=pltpu.CompilerParams(vmem_limit_bytes=60 * 1024 * 1024),
-    )(decay_grid, step_inputs, write_vecs, read_vecs)
+    )(log_decay.T, step_inputs, write_vecs, read_vecs)
     rings = [rings[0]] + [shift_y(rings[s], s) for s in (1, 2, 3)]
 
     queries = [q_same, swapped, swap_x(q_same, 2), swap_x(q_other, 3)]
@@ -439,12 +446,12 @@
     state_shapes = [shape((rows, 128), f32)] * 3
     out_shapes = [shape((LBLK, 4 * HDIM + 128), bf16)] * 4
 
-    def attend_column(state, step, keys, after=()):
+    def attend_column(state, step, keys, after=(), slots=(0, 1, 2, 3)):
         return run(
-            functools.partial(column_attend, step),
-            state_shapes + (out_shapes if step == 2 else []),
+            functools.partial(column_attend, step, slots),
+            state_shapes + (out_shapes[: len(slots)] if step == 2 else []),
             (place, *queries, *state, *keys),
-            flops=4 << 30,
+            flops=len(slots) << 30,
             moved=8 << 20,
             aliases={5: 0, 6: 1, 7: 2},
             after=after,
@@ -486,7 +493,9 @@
     )
     state = attend_column(state, 1, [right], [mixed[0]])
     mixed = [mixed[0]] + [shift_y(mixed[s], s) for s in (1, 2, 3)]
-    *_, o0, o1, o2, o3 = attend_column(state, 2, [shift_y(later_column, 2)], mixed[1:])
+    opposite = shift_y(later_column, 2)
+    *state, o1, o2, o3 = attend_column(state, 2, [opposite], mixed[1:], (1, 2, 3))
+    *_, o0 = attend_column(state, 2, [opposite], [], (0,))
     outs = [o0] + [swap_x(one, s) for s, one in ((1, o1), (2, o2), (3, o3))]
     (mamba_out,) = run(norm_kernel, [shape((LBLK, 4 * SLICE), bf16)], (place, *mixed, gates, gain), after=[o0])
     (attn_out,) = run(merge_kernel, [shape((LBLK, 8 * HDIM), bf16)], (place, *outs))

time: 88.3 us -> 87.5 us (level)
  waiting for transfers between devices: 11.4 us -> 10.3 us
  Pallas kernels: 29.2 us -> 30.2 us
    pallas_call x13 -> x14, Pallas kernels: 26.9 us -> 27.8 us  [run(): pl.pallas_call(body if after else kernel, out_shape=outs, in_specs=[smem]...]
    ppermute x6, waiting for transfers between devices: 5.3 us -> 4.35 us  [swap_x(): return lax.ppermute(vals, 'ctx', [(i, i ^ 4 * step) for i in range(64)])]
  transfers between devices with their start and end apart: 27 -> 27, of which waited for: 7 -> 6; matrix products, arithmetic and copies ran while one was open for 1% -> 0% of each run, Pallas kernels for 25% -> 28%
where the time goes in v1:
time: 87.5 us; the launch traced here: 87.2 us
  starting transfers between devices  42.7 us (49%)
  Pallas kernels  30.2 us (35%)
  waiting for transfers between devices  10.3 us (12%)
  local copies, waits for them, and re-layouts  2.99 us (3%)
  between operations  0.93 us (1%)
    pallas_call x14, Pallas kernels, run(): pl.pallas_call(body if after else kernel, out_shape=outs, in_specs=[smem]...  27.8 us
    ppermute x9, starting transfers between devices, shift_y(): lax.ppermute(vals, 'ctx', [(i, i & ~3 | i + shift & 3) for i in range(64)])  12.5 us
    ppermute x6, starting transfers between devices, up_z(): lax.ppermute(vals, 'ctx', [(i, i + 16 * shift & 63) for i in range(64)])  11.3 us
    ppermute x6, starting transfers between devices, swap_x(): return lax.ppermute(vals, 'ctx', [(i, i ^ 4 * step) for i in range(64)])  11 us
    ppermute x6, starting transfers between devices, shift_x(): lax.ppermute(vals, 'ctx', [(i, i & ~12 | i + 4 * shift & 12) for i in ran...  7.8 us
    ppermute x6, waiting for transfers between devices, up_z(): lax.ppermute(vals, 'ctx', [(i, i + 16 * shift & 63) for i in range(64)])  4.93 us
    ppermute x6, waiting for transfers between devices, swap_x(): return lax.ppermute(vals, 'ctx', [(i, i ^ 4 * step) for i in range(64)])  4.35 us
    pallas_call x1, Pallas kernels, on_device(): pl.pallas_call(pack_kernel, out_shape=[shape((LBLK, WIDTH), bf16)] * 4, i...  2.38 us
  transfers between devices with their start and end apart: 27, of which 6 were waited for; matrix products, arithmetic and copies ran while one was open for 0% of the time, Pallas kernels for 28%

profile of v1, /device:TPU:8, one launch (start us, length us, event | category | flops | bytes accessed | tf_op | source)
XLA Modules:
  0.0 87.2 jit_solution(13657322477925897232)
XLA Ops:
  0.7 1.0 %constant_dynamic-slice_fusion = (bf16[128,512]{1,0:T(8,128)(2,1)S(1)}, bf16[128,512]{1,0:T(8,128)(2,1)S(1)}) fusion(bf16[128,1024]{1,0:T(8,128)(2,1)} %param.17, s32[]{:T(128)S(6)} %select_n.45, s32[]{:T(128)S(6)} %select_n.44), kind=kLoop, calls=%fused_computation.3 | loop fusion | bytes 524296 | tf_op jit(solution)/shard_map/dynamic_slice | solution.py:409
  1.7 0.8 constant_dynamic-slice_fusion.2
  2.6 1.6 %collective-permute-start.3 = (bf16[128,768]{1,0:T(8,128)(2,1)S(1)}, bf16[128,768]{1,0:T(8,128)(2,1)S(1)}, u32[]{:S(2)}, u32[]{:S(2)}) collective-permute-start(bf16[128,768]{1,0:T(8,128)(2,1)S(1)} %pad_maximum_fusion.1), channel_id=1, source_target_pairs={{0,16},{4,20},{8,24},{12,28},{16,0},{20,4},{24,8},{28,12},{32,48},... | collective-permute-start | bytes 589832 | tf_op jit(solution)/shard_map/ppermute | solution.py:387
  4.2 2.4 %shard_map.113 = (bf16[128,1152]{1,0:T(8,128)(2,1)}, bf16[128,1152]{1,0:T(8,128)(2,1)}, bf16[128,1152]{1,0:T(8,128)(2,1)}, bf16[128,1152]{1,0:T(8,128)(2,1)}) custom-call(f32[32,128]{1,0:T(8,128)} %bitcast.7, bf16[128,2048]{1,0:T(8,128)(2,1)} %x.1, bf16[128,512]{1,0:T(8,128)(2,1)} %b.1, bf16[128,512]{1,0:T(8,128)(2,1)} %c.1), custom_call_target="tpu_custom_call" | custom-call | tf_op jit(solution)/shard_map/pallas_call | solution.py:414
  6.7 2.7 %collective-permute-done.3.refs_2_.q1 = bf16[128,768]{1,0:T(8,128)(2,1)S(1)} collective-permute-done((bf16[128,768]{1,0:T(8,128)(2,1)S(1)}, bf16[128,768]{1,0:T(8,128)(2,1)S(1)}, u32[]{:S(2)}, u32[]{:S(2)}) %collective-permute-start.3) | collective-permute-done | bytes 196640 | tf_op jit(solution)/shard_map/ppermute | solution.py:387
  9.3 1.0 %copy-done = bf16[128,1152]{1,0:T(8,128)(2,1)S(1)} copy-done((bf16[128,1152]{1,0:T(8,128)(2,1)S(1)}, bf16[128,1152]{1,0:T(8,128)(2,1)}, u32[]{:S(2)}) %copy-start) | copy-done | bytes 294936
  10.3 0.5 shard_map.114.refs_5_
  10.9 3.4 %collective-permute-start.4 = (bf16[256,256]{1,0:T(8,128)(2,1)S(1)}, bf16[256,256]{1,0:T(8,128)(2,1)S(1)}, u32[]{:S(2)}, u32[]{:S(2)}) collective-permute-start(bf16[256,256]{1,0:T(8,128)(2,1)S(1)} %shard_map.114.refs_5_), channel_id=1, source_target_pairs={{0,128},{4,132},{8,136},{12,140},{16,144},{20,148},{24,152},{28,15... | collective-permute-start | bytes 393224 | tf_op jit(solution)/shard_map/ppermute | solution.py:391
  14.2 1.6 %collective-permute-start = (bf16[128,1152]{1,0:T(8,128)(2,1)}, bf16[128,1152]{1,0:T(8,128)(2,1)S(1)}, u32[]{:S(2)}, u32[]{:S(2)}) collective-permute-start(bf16[128,1152]{1,0:T(8,128)(2,1)} %get-tuple-element.42), channel_id=1, source_target_pairs={{0,4},{4,8},{8,12},{12,0},{16,20},{20,24},{24,28},{28,16},{32,36},... | collective-permute-start | bytes 884744 | tf_op jit(solution)/shard_map/ppermute | solution.py:379
  15.8 0.9 %collective-permute-start.1 = (bf16[128,1152]{1,0:T(8,128)(2,1)}, bf16[128,1152]{1,0:T(8,128)(2,1)S(1)}, u32[]{:S(2)}, u32[]{:S(2)}) collective-permute-start(bf16[128,1152]{1,0:T(8,128)(2,1)} %get-tuple-element.43), channel_id=1, source_target_pairs={{0,8},{4,12},{8,0},{12,4},{16,24},{20,28},{24,16},{28,20},{32,40},... | collective-permute-start | bytes 884744 | tf_op jit(solution)/shard_map/ppermute | solution.py:379
  16.7 2.4 %collective-permute-start.2 = (bf16[128,1152]{1,0:T(8,128)(2,1)}, bf16[128,1152]{1,0:T(8,128)(2,1)S(1)}, u32[]{:S(2)}, u32[]{:S(2)}) collective-permute-start(bf16[128,1152]{1,0:T(8,128)(2,1)} %get-tuple-element.44), channel_id=1, source_target_pairs={{0,12},{4,0},{8,4},{12,8},{16,28},{20,16},{24,20},{28,24},{32,44},... | collective-permute-start | bytes 884744 | tf_op jit(solution)/shard_map/ppermute | solution.py:379
  19.1 1.9 %collective-permute-start.9 = (bf16[256,256]{1,0:T(8,128)(2,1)S(1)}, bf16[256,256]{1,0:T(8,128)(2,1)S(1)}, u32[]{:S(2)}, u32[]{:S(2)}) collective-permute-start(bf16[256,256]{1,0:T(8,128)(2,1)S(1)} %shard_map.114.refs_5_), channel_id=1, source_target_pairs={{0,64},{4,68},{8,72},{12,76},{16,80},{20,84},{24,88},{28,92},{32,9... | collective-permute-start | bytes 393224 | tf_op jit(solution)/shard_map/ppermute | solution.py:391
  21.3 0.8 shard_map.115.refs_6_.refs_5_
  22.1 4.1 %collective-permute-done.9.refs_6_ = bf16[256,256]{1,0:T(8,128)(2,1)S(1)} collective-permute-done((bf16[256,256]{1,0:T(8,128)(2,1)S(1)}, bf16[256,256]{1,0:T(8,128)(2,1)S(1)}, u32[]{:S(2)}, u32[]{:S(2)}) %collective-permute-start.9) | collective-permute-done | bytes 131104 | tf_op jit(solution)/shard_map/ppermute | solution.py:391
  26.2 2.8 %collective-permute-start.11 = (bf16[128,512]{1,0:T(8,128)(2,1)S(1)}, bf16[128,512]{1,0:T(8,128)(2,1)S(1)}, u32[]{:S(2)}, u32[]{:S(2)}) collective-permute-start(bf16[128,512]{1,0:T(8,128)(2,1)S(1)} %get-tuple-element.81), channel_id=1, source_target_pairs={{0,48},{4,52},{8,56},{12,60},{16,32},{20,36},{24,40},{28,44},{32,1... | collective-permute-start | bytes 393224 | tf_op jit(solution)/shard_map/ppermute | solution.py:387
  29.0 1.9 %collective-permute-start.10 = (bf16[128,512]{1,0:T(8,128)(2,1)S(1)}, bf16[128,512]{1,0:T(8,128)(2,1)S(1)}, u32[]{:S(2)}, u32[]{:S(2)}) collective-permute-start(bf16[128,512]{1,0:T(8,128)(2,1)S(1)} %get-tuple-element.80.refs_1_.q0), channel_id=1, source_target_pairs={{0,32},{4,36},{8,40},{12,44},{16,48},{20,52},{24,56},{28,60},{32,0... | collective-permute-start | bytes 393224 | tf_op jit(solution)/shard_map/ppermute | solution.py:387
  30.9 1.6 %collective-permute-start.18 = (bf16[1024,256]{1,0:T(8,128)(2,1)S(1)}, bf16[1024,256]{1,0:T(8,128)(2,1)S(1)}, u32[]{:S(2)}, u32[]{:S(2)}) collective-permute-start(bf16[1024,256]{1,0:T(8,128)(2,1)S(1)} %pad_maximum_fusion.refs_5_), channel_id=1, source_target_pairs={{0,4},{4,8},{8,12},{12,0},{16,20},{20,24},{24,28},{28,16},{32,36},... | collective-permute-start | bytes 1572872 | tf_op jit(solution)/shard_map/ppermute | solution.py:379
  32.5 0.5 collective-permute-start.22
  33.0 1.7 %shard_map.116 = (bf16[272,128]{1,0:T(8,128)(2,1)S(1)}, bf16[272,128]{1,0:T(8,128)(2,1)S(1)}, bf16[272,128]{1,0:T(8,128)(2,1)S(1)}, bf16[272,128]{1,0:T(8,128)(2...) custom-call(s32[4]{0:T(128)S(1)} %pad_add_fusion.refs_0_.place, ...), custom_call_target="tpu_custom_call" | custom-call | flops 629145600 | bytes 2097152 | tf_op jit(solution)/shard_map/pallas_call | solution.py:42
  34.7 0.7 collective-permute-start.6
  35.5 2.3 %collective-permute-start.7 = (bf16[272,128]{1,0:T(8,128)(2,1)S(1)}, bf16[272,128]{1,0:T(8,128)(2,1)S(1)}, u32[]{:S(2)}, u32[]{:S(2)}) collective-permute-start(bf16[272,128]{1,0:T(8,128)(2,1)S(1)} %get-tuple-element.50), channel_id=1, source_target_pairs={{0,32},{4,36},{8,40},{12,44},{16,48},{20,52},{24,56},{28,60},{32,0... | collective-permute-start | bytes 208904 | tf_op jit(solution)/shard_map/ppermute | solution.py:383
  37.7 1.4 %collective-permute-start.8 = (bf16[272,128]{1,0:T(8,128)(2,1)S(1)}, bf16[272,128]{1,0:T(8,128)(2,1)S(1)}, u32[]{:S(2)}, u32[]{:S(2)}) collective-permute-start(bf16[272,128]{1,0:T(8,128)(2,1)S(1)} %get-tuple-element.51), channel_id=1, source_target_pairs={{0,48},{4,52},{8,56},{12,60},{16,0},{20,4},{24,8},{28,12},{32,16},... | collective-permute-start | bytes 208904 | tf_op jit(solution)/shard_map/ppermute | solution.py:383
  39.1 3.7 %shard_map.117 = (f32[2048,128]{1,0:T(8,128)S(1)}, f32[2048,128]{1,0:T(8,128)S(1)}, f32[2048,128]{1,0:T(8,128)S(1)}) custom-call(s32[4]{0:T(128)S(1)} %pad_add_fusion.refs_0_.place, bf16[128,512]{1,0:T(8,128)(2,1)S(1)} %get-tuple-element.80.refs_1_.q0, bf16[128,768]{1,0:T(8,128)(2,1)S(1)} %collective-permute-done.3.refs_2_.q1, ...), custom_call_target="tpu_custom_call" | custom-call | flops 4294967296 | bytes 8388608 | tf_op jit(solution)/shard_map/pallas_call | solution.py:42
  42.8 0.7 shard_map.118
  43.5 3.5 %collective-permute-start.12 = (bf16[272,128]{1,0:T(8,128)(2,1)S(1)}, bf16[272,128]{1,0:T(8,128)(2,1)S(1)}, u32[]{:S(2)}, u32[]{:S(2)}) collective-permute-start(bf16[272,128]{1,0:T(8,128)(2,1)S(1)} %get-tuple-element.53.refs_5_), channel_id=1, source_target_pairs={{0,64},{4,68},{8,72},{12,76},{16,80},{20,84},{24,88},{28,92},{32,9... | collective-permute-start | bytes 208904 | tf_op jit(solution)/shard_map/ppermute | solution.py:391
  47.0 2.5 %collective-permute-start.14 = (bf16[272,128]{1,0:T(8,128)(2,1)S(1)}, bf16[272,128]{1,0:T(8,128)(2,1)S(1)}, u32[]{:S(2)}, u32[]{:S(2)}) collective-permute-start(bf16[272,128]{1,0:T(8,128)(2,1)S(1)} %get-tuple-element.53.refs_5_), channel_id=1, source_target_pairs={{0,192},{4,196},{8,200},{12,204},{16,208},{20,212},{24,216},{28,22... | collective-permute-start | bytes 208904 | tf_op jit(solution)/shard_map/ppermute | solution.py:391
  49.5 2.1 %shard_map.119 = (f32[4,128,512]{2,1,0:T(8,128)S(1)}, f32[4,128,512]{2,1,0:T(8,128)S(1)}) custom-call(s32[4]{0:T(128)S(1)} %pad_add_fusion.refs_0_.place, bf16[4,128,1152]{2,1,0:T(8,128)(2,1)S(1)} %get-tuple-element.45.refs_1_, f32[4,128,512]{2,1,0:T(8,128)S(1)} %get-tuple-element.46.refs_2_, f32[4,256,512]{2,1,0:T(8,128)S(1)} %get-tuple-element.47.refs_3_, ...), custom_call_target="tpu_custom_call" | custom-call | flops 2147483648 | bytes 4194304 | tf_op jit(solution)/shard_map/pallas_call | solution.py:42
  51.5 0.1 collective-permute-start.23
  51.6 0.8 collective-permute-done.13.refs_6_
  52.5 0.7 shard_map.120
  53.3 3.3 %collective-permute-start.16 = (bf16[256,128]{1,0:T(8,128)(2,1)S(1)}, bf16[256,128]{1,0:T(8,128)(2,1)S(1)}, u32[]{:S(2)}, u32[]{:S(2)}) collective-permute-start(bf16[256,128]{1,0:T(8,128)(2,1)S(1)} %get-tuple-element.58), channel_id=1, source_target_pairs={{0,32},{4,36},{8,40},{12,44},{16,48},{20,52},{24,56},{28,60},{32,0... | collective-permute-start | bytes 196616 | tf_op jit(solution)/shard_map/ppermute | solution.py:383
  56.5 0.1 collective-permute-start.17
  56.7 3.9 %shard_map.121 = (f32[2048,128]{1,0:T(8,128)S(1)}, f32[2048,128]{1,0:T(8,128)S(1)}, f32[2048,128]{1,0:T(8,128)S(1)}) custom-call(s32[4]{0:T(128)S(1)} %pad_add_fusion.refs_0_.place, bf16[128,512]{1,0:T(8,128)(2,1)S(1)} %get-tuple-element.80.refs_1_.q0, ...), custom_call_target="tpu_custom_call", output_to_operand_aliasing={{0}: (5, {}), {1}: (6, {}), {2}: (7, {})} | custom-call | flops 4294967296 | bytes 8388608 | tf_op jit(solution)/shard_map/pallas_call | solution.py:42
  60.6 0.2 collective-permute-done.17.refs_7_
  60.8 1.0 %shard_map.122 = (bf16[128,512]{1,0:T(8,128)(2,1)S(1)}, bf16[128,512]{1,0:T(8,128)(2,1)S(1)}, bf16[128,512]{1,0:T(8,128)(2,1)S(1)}, bf16[128,512]{1,0:T(8,128)(2,1)S(1)}) custom-call(s32[4]{0:T(128)S(1)} %pad_add_fusion.refs_0_.place, bf16[4,128,1152]{2,1,0:T(8,128)(2,1)S(1)} %get-tuple-element.45.refs_1_, ...), custom_call_target="tpu_custom_call" | custom-call | flops 1000000 | bytes 1000000 | tf_op jit(solution)/shard_map/pallas_call | solution.py:42
  61.8 2.2 %collective-permute-start.19 = (bf16[128,512]{1,0:T(8,128)(2,1)S(1)}, bf16[128,512]{1,0:T(8,128)(2,1)S(1)}, u32[]{:S(2)}, u32[]{:S(2)}) collective-permute-start(bf16[128,512]{1,0:T(8,128)(2,1)S(1)} %get-tuple-element.64), channel_id=1, source_target_pairs={{0,4},{4,8},{8,12},{12,0},{16,20},{20,24},{24,28},{28,16},{32,36},... | collective-permute-start | bytes 393224 | tf_op jit(solution)/shard_map/ppermute | solution.py:379
  64.0 1.8 %collective-permute-start.20 = (bf16[128,512]{1,0:T(8,128)(2,1)S(1)}, bf16[128,512]{1,0:T(8,128)(2,1)S(1)}, u32[]{:S(2)}, u32[]{:S(2)}) collective-permute-start(bf16[128,512]{1,0:T(8,128)(2,1)S(1)} %get-tuple-element.65), channel_id=1, source_target_pairs={{0,8},{4,12},{8,0},{12,4},{16,24},{20,28},{24,16},{28,20},{32,40},... | collective-permute-start | bytes 393224 | tf_op jit(solution)/shard_map/ppermute | solution.py:379
  65.8 1.4 %collective-permute-start.21 = (bf16[128,512]{1,0:T(8,128)(2,1)S(1)}, bf16[128,512]{1,0:T(8,128)(2,1)S(1)}, u32[]{:S(2)}, u32[]{:S(2)}) collective-permute-start(bf16[128,512]{1,0:T(8,128)(2,1)S(1)} %get-tuple-element.66), channel_id=1, source_target_pairs={{0,12},{4,0},{8,4},{12,8},{16,28},{20,16},{24,20},{28,24},{32,44},... | collective-permute-start | bytes 393224 | tf_op jit(solution)/shard_map/ppermute | solution.py:379
  67.2 3.9 %shard_map.123 = (f32[2048,128]{1,0:T(8,128)S(1)}, f32[2048,128]{1,0:T(8,128)S(1)}, f32[2048,128]{1,0:T(8,128)S(1)}) custom-call(s32[4]{0:T(128)S(1)} %pad_add_fusion.refs_0_.place, bf16[128,512]{1,0:T(8,128)(2,1)S(1)} %get-tuple-element.80.refs_1_.q0, ...), custom_call_target="tpu_custom_call", output_to_operand_aliasing={{0}: (5, {}), {1}: (6, {}), {2}: (7, {})} | custom-call | flops 4294967296 | bytes 8388608 | tf_op jit(solution)/shard_map/pallas_call | solution.py:42
  71.1 0.8 collective-permute-done.21.refs_11_.refs_4_
  71.9 3.3 %shard_map.124 = (f32[2048,128]{1,0:T(8,128)S(1)}, f32[2048,128]{1,0:T(8,128)S(1)}, f32[2048,128]{1,0:T(8,128)S(1)}, bf16[128,640]{1,0:T(8,128)(2,1)S(1)}, bf16[...) custom-call(s32[4]{0:T(128)S(1)} %pad_add_fusion.refs_0_.place, ...), custom_call_target="tpu_custom_call", output_to_operand_aliasing={{0}: (5, {}), {1}: (6, {}), {2}: (7, {})} | custom-call | flops 3221225472 | bytes 8388608 | tf_op jit(solution)/shard_map/pallas_call | solution.py:42
  75.2 1.0 %collective-permute-start.24 = (bf16[128,640]{1,0:T(8,128)(2,1)S(1)}, bf16[128,640]{1,0:T(8,128)(2,1)S(1)}, u32[]{:S(2)}, u32[]{:S(2)}) collective-permute-start(bf16[128,640]{1,0:T(8,128)(2,1)S(1)} %get-tuple-element.77), channel_id=1, source_target_pairs={{0,16},{4,20},{8,24},{12,28},{16,0},{20,4},{24,8},{28,12},{32,48},... | collective-permute-start | bytes 491528 | tf_op jit(solution)/shard_map/ppermute | solution.py:387
  76.2 2.1 %collective-permute-start.25 = (bf16[128,640]{1,0:T(8,128)(2,1)S(1)}, bf16[128,640]{1,0:T(8,128)(2,1)S(1)}, u32[]{:S(2)}, u32[]{:S(2)}) collective-permute-start(bf16[128,640]{1,0:T(8,128)(2,1)S(1)} %get-tuple-element.78), channel_id=1, source_target_pairs={{0,32},{4,36},{8,40},{12,44},{16,48},{20,52},{24,56},{28,60},{32,0... | collective-permute-start | bytes 491528 | tf_op jit(solution)/shard_map/ppermute | solution.py:387
  78.3 1.7 %collective-permute-start.26 = (bf16[128,640]{1,0:T(8,128)(2,1)S(1)}, bf16[128,640]{1,0:T(8,128)(2,1)S(1)}, u32[]{:S(2)}, u32[]{:S(2)}) collective-permute-start(bf16[128,640]{1,0:T(8,128)(2,1)S(1)} %get-tuple-element.79), channel_id=1, source_target_pairs={{0,48},{4,52},{8,56},{12,60},{16,32},{20,36},{24,40},{28,44},{32,1... | collective-permute-start | bytes 491528 | tf_op jit(solution)/shard_map/ppermute | solution.py:387
  80.0 1.8 %shard_map.125 = (f32[2048,128]{1,0:T(8,128)S(1)}, f32[2048,128]{1,0:T(8,128)S(1)}, f32[2048,128]{1,0:T(8,128)S(1)}, bf16[128,640]{1,0:T(8,128)(2,1)S(1)}) custom-call(s32[4]{0:T(128)S(1)} %pad_add_fusion.refs_0_.place, bf16[128,512]{1,0:T(8,128)(2,1)S(1)} %get-tuple-element.80.refs_1_.q0, ...), custom_call_target="tpu_custom_call", output_to_operand_aliasing={{0}: (5, {}), {1}: (6, {}), {2}: (7, {})} | custom-call | flops 1073741824 | bytes 8388608 | tf_op jit(solution)/shard_map/pallas_call | solution.py:42
  81.8 1.7 %shard_map.126 = bf16[128,2048]{1,0:T(8,128)(2,1)} custom-call(s32[4]{0:T(128)S(1)} %pad_add_fusion.refs_0_.place, bf16[128,512]{1,0:T(8,128)(2,1)S(1)} %get-tuple-element.63.refs_9_.refs_1_, bf16[128,512]{1,0:T(8,128)(2,1)S(1)} %collective-permute-done.19.refs_9_.refs_2_, bf16[128,512]{1,0:T(8,128)(2,1)S(1)} %collective-permute-done.20.refs_10_.refs_3_, ...), custom_call_target="tpu_custom_call" | custom-call | flops 1000000 | bytes 1000000 | tf_op jit(solution)/shard_map/pallas_call | solution.py:42
  83.5 1.6 %collective-permute-done.26.o3 = bf16[128,640]{1,0:T(8,128)(2,1)S(1)} collective-permute-done((bf16[128,640]{1,0:T(8,128)(2,1)S(1)}, bf16[128,640]{1,0:T(8,128)(2,1)S(1)}, u32[]{:S(2)}, u32[]{:S(2)}) %collective-permute-start.26) | collective-permute-done | bytes 163872 | tf_op jit(solution)/shard_map/ppermute | solution.py:387
  85.1 2.1 %shard_map.127 = bf16[128,1024]{1,0:T(8,128)(2,1)} custom-call(s32[4]{0:T(128)S(1)} %pad_add_fusion.refs_0_.place, bf16[128,640]{1,0:T(8,128)(2,1)S(1)} %get-tuple-element.76.refs_7_.o0, bf16[128,640]{1,0:T(8,128)(2,1)S(1)} %collective-permute-done.24.o1, bf16[128,640]{1,0:T(8,128)(2,1)S(1)} %collective-permute-done.25.o2, ...), custom_call_target="tpu_custom_call" | custom-call | flops 1000000 | bytes 1000000 | tf_op jit(solution)/shard_map/pallas_call | solution.py:42
  (39 shorter events, 0.5 us)
Async XLA Ops:
  0.6 20.5 %copy-start.4 = (f32[32]{0:T(128)S(1)}, f32[32]{0:T(128)}, u32[]{:S(2)}) copy-start(f32[32]{0:T(128)} %param.15) | copy-start | bytes 388
  0.6 20.6 %copy-start.2 = (bf16[128,2048]{1,0:T(8,128)(2,1)S(1)}, bf16[128,2048]{1,0:T(8,128)(2,1)}, u32[]{:S(2)}) copy-start(bf16[128,2048]{1,0:T(8,128)(2,1)} %gate.1) | copy-start | bytes 1572868
  2.6 6.7 %collective-permute-start.3 = (bf16[128,768]{1,0:T(8,128)(2,1)S(1)}, bf16[128,768]{1,0:T(8,128)(2,1)S(1)}, u32[]{:S(2)}, u32[]{:S(2)}) collective-permute-start(bf16[128,768]{1,0:T(8,128)(2,1)S(1)} %pad_maximum_fusion.1), channel_id=1, source_target_pairs={{0,16},{4,20},{8,24},{12,28},{16,0},{20,4},{24,8},{28,12},{32,48},... | collective-permute-start | bytes 589832 | tf_op jit(solution)/shard_map/ppermute | solution.py:387
  9.3 1.0 %copy-start = (bf16[128,1152]{1,0:T(8,128)(2,1)S(1)}, bf16[128,1152]{1,0:T(8,128)(2,1)}, u32[]{:S(2)}) copy-start(bf16[128,1152]{1,0:T(8,128)(2,1)} %get-tuple-element.41.refs_3_.refs_1_) | copy-start | bytes 884740
  10.3 22.7 %copy-start.1 = (bf16[128,1152]{1,0:T(8,128)(2,1)S(1)}, bf16[128,1152]{1,0:T(8,128)(2,1)}, u32[]{:S(2)}) copy-start(bf16[128,1152]{1,0:T(8,128)(2,1)} %get-tuple-element.41.refs_3_.refs_1_) | copy-start | bytes 884740
  10.9 10.2 %collective-permute-start.4 = (bf16[256,256]{1,0:T(8,128)(2,1)S(1)}, bf16[256,256]{1,0:T(8,128)(2,1)S(1)}, u32[]{:S(2)}, u32[]{:S(2)}) collective-permute-start(bf16[256,256]{1,0:T(8,128)(2,1)S(1)} %shard_map.114.refs_5_), channel_id=1, source_target_pairs={{0,128},{4,132},{8,136},{12,140},{16,144},{20,148},{24,152},{28,15... | collective-permute-start | bytes 393224 | tf_op jit(solution)/shard_map/ppermute | solution.py:391
  14.2 16.7 %collective-permute-start = (bf16[128,1152]{1,0:T(8,128)(2,1)}, bf16[128,1152]{1,0:T(8,128)(2,1)S(1)}, u32[]{:S(2)}, u32[]{:S(2)}) collective-permute-start(bf16[128,1152]{1,0:T(8,128)(2,1)} %get-tuple-element.42), channel_id=1, source_target_pairs={{0,4},{4,8},{8,12},{12,0},{16,20},{20,24},{24,28},{28,16},{32,36},... | collective-permute-start | bytes 884744 | tf_op jit(solution)/shard_map/ppermute | solution.py:379
  15.8 16.8 %collective-permute-start.1 = (bf16[128,1152]{1,0:T(8,128)(2,1)}, bf16[128,1152]{1,0:T(8,128)(2,1)S(1)}, u32[]{:S(2)}, u32[]{:S(2)}) collective-permute-start(bf16[128,1152]{1,0:T(8,128)(2,1)} %get-tuple-element.43), channel_id=1, source_target_pairs={{0,8},{4,12},{8,0},{12,4},{16,24},{20,28},{24,16},{28,20},{32,40},... | collective-permute-start | bytes 884744 | tf_op jit(solution)/shard_map/ppermute | solution.py:379
  16.7 16.3 %collective-permute-start.2 = (bf16[128,1152]{1,0:T(8,128)(2,1)}, bf16[128,1152]{1,0:T(8,128)(2,1)S(1)}, u32[]{:S(2)}, u32[]{:S(2)}) collective-permute-start(bf16[128,1152]{1,0:T(8,128)(2,1)} %get-tuple-element.44), channel_id=1, source_target_pairs={{0,12},{4,0},{8,4},{12,8},{16,28},{20,16},{24,20},{28,24},{32,44},... | collective-permute-start | bytes 884744 | tf_op jit(solution)/shard_map/ppermute | solution.py:379
  19.1 7.1 %collective-permute-start.9 = (bf16[256,256]{1,0:T(8,128)(2,1)S(1)}, bf16[256,256]{1,0:T(8,128)(2,1)S(1)}, u32[]{:S(2)}, u32[]{:S(2)}) collective-permute-start(bf16[256,256]{1,0:T(8,128)(2,1)S(1)} %shard_map.114.refs_5_), channel_id=1, source_target_pairs={{0,64},{4,68},{8,72},{12,76},{16,80},{20,84},{24,88},{28,92},{32,9... | collective-permute-start | bytes 393224 | tf_op jit(solution)/shard_map/ppermute | solution.py:391
  21.1 7.9 %collective-permute-start.5 = (bf16[256,256]{1,0:T(8,128)(2,1)S(1)}, bf16[256,256]{1,0:T(8,128)(2,1)S(1)}, u32[]{:S(2)}, u32[]{:S(2)}) collective-permute-start(bf16[256,256]{1,0:T(8,128)(2,1)S(1)} %collective-permute-done.4.refs_7_), channel_id=1, source_target_pairs={{0,64},{4,68},{8,72},{12,76},{16,80},{20,84},{24,88},{28,92},{32,9... | collective-permute-start | bytes 393224 | tf_op jit(solution)/shard_map/ppermute | solution.py:391
  26.2 11.5 %collective-permute-start.11 = (bf16[128,512]{1,0:T(8,128)(2,1)S(1)}, bf16[128,512]{1,0:T(8,128)(2,1)S(1)}, u32[]{:S(2)}, u32[]{:S(2)}) collective-permute-start(bf16[128,512]{1,0:T(8,128)(2,1)S(1)} %get-tuple-element.81), channel_id=1, source_target_pairs={{0,48},{4,52},{8,56},{12,60},{16,32},{20,36},{24,40},{28,44},{32,1... | collective-permute-start | bytes 393224 | tf_op jit(solution)/shard_map/ppermute | solution.py:387
  29.0 6.5 %collective-permute-start.10 = (bf16[128,512]{1,0:T(8,128)(2,1)S(1)}, bf16[128,512]{1,0:T(8,128)(2,1)S(1)}, u32[]{:S(2)}, u32[]{:S(2)}) collective-permute-start(bf16[128,512]{1,0:T(8,128)(2,1)S(1)} %get-tuple-element.80.refs_1_.q0), channel_id=1, source_target_pairs={{0,32},{4,36},{8,40},{12,44},{16,48},{20,52},{24,56},{28,60},{32,0... | collective-permute-start | bytes 393224 | tf_op jit(solution)/shard_map/ppermute | solution.py:387
  30.9 25.6 %collective-permute-start.18 = (bf16[1024,256]{1,0:T(8,128)(2,1)S(1)}, bf16[1024,256]{1,0:T(8,128)(2,1)S(1)}, u32[]{:S(2)}, u32[]{:S(2)}) collective-permute-start(bf16[1024,256]{1,0:T(8,128)(2,1)S(1)} %pad_maximum_fusion.refs_5_), channel_id=1, source_target_pairs={{0,4},{4,8},{8,12},{12,0},{16,20},{20,24},{24,28},{28,16},{32,36},... | collective-permute-start | bytes 1572872 | tf_op jit(solution)/shard_map/ppermute | solution.py:379
  32.5 34.6 %collective-permute-start.22 = (bf16[1024,256]{1,0:T(8,128)(2,1)S(1)}, bf16[1024,256]{1,0:T(8,128)(2,1)S(1)}, u32[]{:S(2)}, u32[]{:S(2)}) collective-permute-start(bf16[1024,256]{1,0:T(8,128)(2,1)S(1)} %pad_maximum_fusion.refs_5_), channel_id=1, source_target_pairs={{0,12},{4,0},{8,4},{12,8},{16,28},{20,16},{24,20},{28,24},{32,44},... | collective-permute-start | bytes 1572872 | tf_op jit(solution)/shard_map/ppermute | solution.py:379
  34.7 8.0 %collective-permute-start.6 = (bf16[272,128]{1,0:T(8,128)(2,1)S(1)}, bf16[272,128]{1,0:T(8,128)(2,1)S(1)}, u32[]{:S(2)}, u32[]{:S(2)}) collective-permute-start(bf16[272,128]{1,0:T(8,128)(2,1)S(1)} %get-tuple-element.49), channel_id=1, source_target_pairs={{0,16},{4,20},{8,24},{12,28},{16,32},{20,36},{24,40},{28,44},{32,4... | collective-permute-start | bytes 208904 | tf_op jit(solution)/shard_map/ppermute | solution.py:383
  35.5 7.3 %collective-permute-start.7 = (bf16[272,128]{1,0:T(8,128)(2,1)S(1)}, bf16[272,128]{1,0:T(8,128)(2,1)S(1)}, u32[]{:S(2)}, u32[]{:S(2)}) collective-permute-start(bf16[272,128]{1,0:T(8,128)(2,1)S(1)} %get-tuple-element.50), channel_id=1, source_target_pairs={{0,32},{4,36},{8,40},{12,44},{16,48},{20,52},{24,56},{28,60},{32,0... | collective-permute-start | bytes 208904 | tf_op jit(solution)/shard_map/ppermute | solution.py:383
  37.7 5.1 %collective-permute-start.8 = (bf16[272,128]{1,0:T(8,128)(2,1)S(1)}, bf16[272,128]{1,0:T(8,128)(2,1)S(1)}, u32[]{:S(2)}, u32[]{:S(2)}) collective-permute-start(bf16[272,128]{1,0:T(8,128)(2,1)S(1)} %get-tuple-element.51), channel_id=1, source_target_pairs={{0,48},{4,52},{8,56},{12,60},{16,0},{20,4},{24,8},{28,12},{32,16},... | collective-permute-start | bytes 208904 | tf_op jit(solution)/shard_map/ppermute | solution.py:383
  43.5 8.1 %collective-permute-start.12 = (bf16[272,128]{1,0:T(8,128)(2,1)S(1)}, bf16[272,128]{1,0:T(8,128)(2,1)S(1)}, u32[]{:S(2)}, u32[]{:S(2)}) collective-permute-start(bf16[272,128]{1,0:T(8,128)(2,1)S(1)} %get-tuple-element.53.refs_5_), channel_id=1, source_target_pairs={{0,64},{4,68},{8,72},{12,76},{16,80},{20,84},{24,88},{28,92},{32,9... | collective-permute-start | bytes 208904 | tf_op jit(solution)/shard_map/ppermute | solution.py:391
  47.0 5.5 %collective-permute-start.13 = (bf16[272,128]{1,0:T(8,128)(2,1)S(1)}, bf16[272,128]{1,0:T(8,128)(2,1)S(1)}, u32[]{:S(2)}, u32[]{:S(2)}) collective-permute-start(bf16[272,128]{1,0:T(8,128)(2,1)S(1)} %get-tuple-element.53.refs_5_), channel_id=1, source_target_pairs={{0,128},{4,132},{8,136},{12,140},{16,144},{20,148},{24,152},{28,15... | collective-permute-start | bytes 208904 | tf_op jit(solution)/shard_map/ppermute | solution.py:391
  47.0 5.5 %collective-permute-start.14 = (bf16[272,128]{1,0:T(8,128)(2,1)S(1)}, bf16[272,128]{1,0:T(8,128)(2,1)S(1)}, u32[]{:S(2)}, u32[]{:S(2)}) collective-permute-start(bf16[272,128]{1,0:T(8,128)(2,1)S(1)} %get-tuple-element.53.refs_5_), channel_id=1, source_target_pairs={{0,192},{4,196},{8,200},{12,204},{16,208},{20,212},{24,216},{28,22... | collective-permute-start | bytes 208904 | tf_op jit(solution)/shard_map/ppermute | solution.py:391
  51.5 19.5 %collective-permute-start.23 = (bf16[1024,256]{1,0:T(8,128)(2,1)S(1)}, bf16[1024,256]{1,0:T(8,128)(2,1)S(1)}, u32[]{:S(2)}, u32[]{:S(2)}) collective-permute-start(bf16[1024,256]{1,0:T(8,128)(2,1)S(1)} %get-tuple-element.72), channel_id=1, source_target_pairs={{0,8},{4,12},{8,0},{12,4},{16,24},{20,28},{24,16},{28,20},{32,40},... | collective-permute-start | bytes 1572872 | tf_op jit(solution)/shard_map/ppermute | solution.py:379
  53.2 7.4 %collective-permute-start.15 = (bf16[256,128]{1,0:T(8,128)(2,1)S(1)}, bf16[256,128]{1,0:T(8,128)(2,1)S(1)}, u32[]{:S(2)}, u32[]{:S(2)}) collective-permute-start(bf16[256,128]{1,0:T(8,128)(2,1)S(1)} %get-tuple-element.57), channel_id=1, source_target_pairs={{0,16},{4,20},{8,24},{12,28},{16,32},{20,36},{24,40},{28,44},{32,4... | collective-permute-start | bytes 196616 | tf_op jit(solution)/shard_map/ppermute | solution.py:383
  53.3 7.3 %collective-permute-start.16 = (bf16[256,128]{1,0:T(8,128)(2,1)S(1)}, bf16[256,128]{1,0:T(8,128)(2,1)S(1)}, u32[]{:S(2)}, u32[]{:S(2)}) collective-permute-start(bf16[256,128]{1,0:T(8,128)(2,1)S(1)} %get-tuple-element.58), channel_id=1, source_target_pairs={{0,32},{4,36},{8,40},{12,44},{16,48},{20,52},{24,56},{28,60},{32,0... | collective-permute-start | bytes 196616 | tf_op jit(solution)/shard_map/ppermute | solution.py:383
  56.5 4.3 %collective-permute-start.17 = (bf16[256,128]{1,0:T(8,128)(2,1)S(1)}, bf16[256,128]{1,0:T(8,128)(2,1)S(1)}, u32[]{:S(2)}, u32[]{:S(2)}) collective-permute-start(bf16[256,128]{1,0:T(8,128)(2,1)S(1)} %get-tuple-element.59), channel_id=1, source_target_pairs={{0,48},{4,52},{8,56},{12,60},{16,0},{20,4},{24,8},{28,12},{32,16},... | collective-permute-start | bytes 196616 | tf_op jit(solution)/shard_map/ppermute | solution.py:383
  61.8 9.3 %collective-permute-start.19 = (bf16[128,512]{1,0:T(8,128)(2,1)S(1)}, bf16[128,512]{1,0:T(8,128)(2,1)S(1)}, u32[]{:S(2)}, u32[]{:S(2)}) collective-permute-start(bf16[128,512]{1,0:T(8,128)(2,1)S(1)} %get-tuple-element.64), channel_id=1, source_target_pairs={{0,4},{4,8},{8,12},{12,0},{16,20},{20,24},{24,28},{28,16},{32,36},... | collective-permute-start | bytes 393224 | tf_op jit(solution)/shard_map/ppermute | solution.py:379
  64.0 7.1 %collective-permute-start.20 = (bf16[128,512]{1,0:T(8,128)(2,1)S(1)}, bf16[128,512]{1,0:T(8,128)(2,1)S(1)}, u32[]{:S(2)}, u32[]{:S(2)}) collective-permute-start(bf16[128,512]{1,0:T(8,128)(2,1)S(1)} %get-tuple-element.65), channel_id=1, source_target_pairs={{0,8},{4,12},{8,0},{12,4},{16,24},{20,28},{24,16},{28,20},{32,40},... | collective-permute-start | bytes 393224 | tf_op jit(solution)/shard_map/ppermute | solution.py:379
  65.8 6.1 %collective-permute-start.21 = (bf16[128,512]{1,0:T(8,128)(2,1)S(1)}, bf16[128,512]{1,0:T(8,128)(2,1)S(1)}, u32[]{:S(2)}, u32[]{:S(2)}) collective-permute-start(bf16[128,512]{1,0:T(8,128)(2,1)S(1)} %get-tuple-element.66), channel_id=1, source_target_pairs={{0,12},{4,0},{8,4},{12,8},{16,28},{20,16},{24,20},{28,24},{32,44},... | collective-permute-start | bytes 393224 | tf_op jit(solution)/shard_map/ppermute | solution.py:379
  75.2 8.3 %collective-permute-start.24 = (bf16[128,640]{1,0:T(8,128)(2,1)S(1)}, bf16[128,640]{1,0:T(8,128)(2,1)S(1)}, u32[]{:S(2)}, u32[]{:S(2)}) collective-permute-start(bf16[128,640]{1,0:T(8,128)(2,1)S(1)} %get-tuple-element.77), channel_id=1, source_target_pairs={{0,16},{4,20},{8,24},{12,28},{16,0},{20,4},{24,8},{28,12},{32,48},... | collective-permute-start | bytes 491528 | tf_op jit(solution)/shard_map/ppermute | solution.py:387
  76.2 7.3 %collective-permute-start.25 = (bf16[128,640]{1,0:T(8,128)(2,1)S(1)}, bf16[128,640]{1,0:T(8,128)(2,1)S(1)}, u32[]{:S(2)}, u32[]{:S(2)}) collective-permute-start(bf16[128,640]{1,0:T(8,128)(2,1)S(1)} %get-tuple-element.78), channel_id=1, source_target_pairs={{0,32},{4,36},{8,40},{12,44},{16,48},{20,52},{24,56},{28,60},{32,0... | collective-permute-start | bytes 491528 | tf_op jit(solution)/shard_map/ppermute | solution.py:387
  78.3 6.8 %collective-permute-start.26 = (bf16[128,640]{1,0:T(8,128)(2,1)S(1)}, bf16[128,640]{1,0:T(8,128)(2,1)S(1)}, u32[]{:S(2)}, u32[]{:S(2)}) collective-permute-start(bf16[128,640]{1,0:T(8,128)(2,1)S(1)} %get-tuple-element.79), channel_id=1, source_target_pairs={{0,48},{4,52},{8,56},{12,60},{16,32},{20,36},{24,40},{28,44},{32,1... | collective-permute-start | bytes 491528 | tf_op jit(solution)/shard_map/ppermute | solution.py:387
  80.0 1.8 %copy-start.3 = (f32[2048]{0:T(1024)S(1)}, f32[2048]{0:T(1024)}, u32[]{:S(2)}) copy-start(f32[2048]{0:T(1024)} %param.16) | copy-start | bytes 24580
